TPU v7x, 512 devices: a whole 4x4x16 slice. The times are simulated.
512 devices in a mesh: rec: 32 (over x_hi, z), lig: 16 (over y, x_lo, core).
Axes of the slice: x: 4 (x_hi: 2, x_lo: 2; x = x_hi * 2 + x_lo), y: 4, z: 16, core: 2. Of those that a mesh axis runs over, the one named last changes fastest.
Arguments:
- receptor: bfloat16 [32, 4, 32, 1024], P('rec', None, 'lig'), may hold values from -6 to 6
- ligand_pool: bfloat16 [16, 32, 2, 4, 32, 1024], P('lig', 'rec'), may hold values from -6 to 6
- channel_weight: float32 [4], replicated, may hold values from -3 to 3
- owners: int32 [16, 2], P('lig'), may hold values from 0 to 31
- rotations: int32 [16, 2, 2], P('lig'), may hold values from 0 to 1, each once within a row
Outputs:
- scores: bfloat16 [32, 16, 2, 2, 32, 1024], P('rec', 'lig')
- best: float32 [32, 16, 2, 2], P('rec', 'lig')
- best_all: float32 [16, 2, 2], P('lig')
Inputs may be any that keep to these rules, and one draw needn't show every extreme that they name: `rotations`: each row of the last dimension holds every grid of the set once.
All inputs are finite; a program needn't handle non-finite values.
Results may differ from a plain program's by a relative error of at most 0.0049.
Values may be sent and summed in bfloat16 or wider, within the bound.
A program may use at most 64 MiB of HBM per device.

v0:
```python
import jax
import jax.numpy as jnp
from jax import lax
from jax.sharding import PartitionSpec as P

HIGH = lax.Precision.HIGHEST


def spread(block, axis, holder):
    block = jnp.where(lax.axis_index(axis) == holder, block, jnp.zeros_like(block))
    return lax.psum(block, axis)


def trig_tables(size):
    index = jnp.arange(size, dtype=jnp.int32)
    phase = index[:, None] * index[None, :] % size
    angle = phase.astype(jnp.float32) * (2.0 * jnp.pi / size)
    return (jnp.cos(angle), jnp.sin(angle))


def apply_rows(weight, stack):
    return jnp.einsum("ab,nbm->nam", weight, stack, precision=HIGH)


def cycle_axes(stack, size):
    count = stack.shape[0]
    parts = stack.shape[1] // size
    shaped = stack.reshape(count, parts, size, size, size)
    return shaped.transpose(0, 1, 3, 4, 2).reshape(count, parts * size, size * size)


def forward_full(grids, cosine, sine):
    size = cosine.shape[0]
    real_in = jnp.concatenate([cosine, -sine], 0)
    both = jnp.concatenate(
        [jnp.concatenate([cosine, sine], 1), jnp.concatenate([-sine, cosine], 1)], 0
    )
    stack = cycle_axes(apply_rows(real_in, grids), size)
    stack = cycle_axes(apply_rows(both, stack), size)
    return cycle_axes(apply_rows(both, stack), size)


def inverse_real(stack, cosine, sine):
    size = cosine.shape[0]
    both = jnp.concatenate(
        [jnp.concatenate([cosine, -sine], 1), jnp.concatenate([sine, cosine], 1)], 0
    )
    real_out = jnp.concatenate([cosine, -sine], 1)
    stack = cycle_axes(apply_rows(both, stack), size)
    stack = cycle_axes(apply_rows(both, stack), size)
    return cycle_axes(apply_rows(real_out, stack), size)


def receptor_spectrum(receptor, cosine, sine):
    whole = lax.all_gather(receptor, "lig", axis=2, tiled=True)
    return forward_full(whole[0].astype(jnp.float32), cosine, sine)


def round_to_half(values):
    return lax.optimization_barrier(values.astype(jnp.bfloat16)).astype(jnp.float32)


def round_spectra(picked, cosine, sine):
    poses = picked.shape[0]
    whole = jnp.stack(
        [forward_full(picked[pose].astype(jnp.float32), cosine, sine) for pose in range(poses)], 0
    )
    return round_to_half(whole)


def on_device(receptor, ligand_pool, channel_weight, owners, rotations):
    size = ligand_pool.shape[4]
    channels = ligand_pool.shape[3]
    poses = ligand_pool.shape[2]
    rounds = owners.shape[1]
    cosine, sine = trig_tables(size)
    scale = 1.0 / (float(size) ** 3 * float(channels * size**3) ** 0.5)
    spectrum = receptor_spectrum(receptor, cosine, sine)
    weighted = spectrum * channel_weight[:, None, None]
    rec_real = weighted[:, :size]
    rec_imag = weighted[:, size:]
    score_rounds = []
    best_rounds = []
    for step in range(rounds):
        grids = spread(ligand_pool, "rec", owners[0, step])
        picked = jnp.take(grids[0, 0], rotations[0, step], axis=0)
        spectra = round_spectra(picked, cosine, sine)
        round_scores = []
        for pose in range(poses):
            lig_real = spectra[pose, :, :size]
            lig_imag = spectra[pose, :, size:]
            prod_real = jnp.sum(rec_real * lig_real + rec_imag * lig_imag, axis=0)
            prod_imag = jnp.sum(rec_real * lig_imag - rec_imag * lig_real, axis=0)
            product = jnp.concatenate([prod_real, prod_imag], 0)[None]
            score_map = inverse_real(product, cosine, sine)[0] * scale
            round_scores.append(score_map)
        stacked = jnp.stack(round_scores, 0)
        score_rounds.append(stacked)
        best_rounds.append(jnp.max(stacked.reshape(poses, -1), axis=1))
    all_scores = jnp.stack(score_rounds, 0)
    best = jnp.stack(best_rounds, 0)
    best_all = lax.pmax(best, "rec")
    scores = all_scores.astype(jnp.bfloat16)[None, None]
    return (scores, best[None, None], best_all[None])


def solution(mesh):
    in_specs = (
        P("rec", None, "lig", None),
        P("lig", "rec", None, None, None, None),
        P(),
        P("lig", None),
        P("lig", None, None),
    )
    out_specs = (
        P("rec", "lig", None, None, None, None),
        P("rec", "lig", None, None),
        P("lig", None, None),
    )
    return jax.shard_map(
        on_device, mesh=mesh, in_specs=in_specs, out_specs=out_specs, check_vma=False
    )
```

profile of v0, /device:TPU:24, one launch (start us, length us, event | category | flops | bytes accessed | tf_op | source)
XLA Modules:
  0.0 607.0 jit_solution(15420623183922122610)
XLA Ops:
  13.0 19.2 %all_gather.3 = bf16[1,4,32,1024]{3,1,0,2:T(4,128)(2,1)S(1)} all-gather(bf16[1,4,2,1024]{3,1,0,2:T(4,128)(2,1)S(1)} %copy.73), channel_id=1, replica_groups=mesh['rec'=32,'lig'=16] {'lig'}, dimensions={2}, use_global_device_ids=true | all-gather | bytes 278528 | tf_op jit(solution)/shard_map/all_gather | solution.py:55
  35.6 5.7 copy.75
  41.2 3.8 reshape.342
  48.8 5.7 copy.77
  54.5 3.7 reshape.344
  62.1 5.7 copy.79
  67.8 3.8 reshape.346
  72.9 246.4 %all-reduce.3.cloned.1.call-done = (bf16[2,4,32,1024]{3,2,1,0:T(8,128)(2,1)}, bf16[2,4,32,1024]{3,2,1,0:T(8,128)(2,1)}) async-done(((bf16[2,4,32,1024]{3,2,1,0:T(8,128)(2,1)}, bf16[2,4,32,1024]{3,2,1,0:T(8,128)(2,1)}), (bf16[2,4,32,1024]{3,2,1,0:T(8,128)(2,1)}, bf16[2,4,32,1024]{3,2,1,0:T(8,128)(2,1)})) %all-reduce.3.cloned.1.call-update) | async-done | bytes 1048592 | tf_op jit(solution)/shard_map/psum | solution.py:11
  330.2 5.7 copy.85
  335.9 3.7 reshape.353
  343.5 5.7 copy.87
  349.1 3.7 reshape.355
  360.9 4.2 stack_reshape.17
  365.1 3.9 reshape.347
  369.1 5.7 copy.80
  374.7 4.1 reshape.348
  382.7 5.7 copy.82
  388.4 3.7 reshape.350
  405.1 3.9 reshape.370
  409.0 5.7 copy.101
  414.7 4.7 reshape.371
  422.8 3.9 reshape.372
  426.7 5.7 copy.103
  432.4 4.6 reshape.373
  443.7 4.8 copy.105
  448.5 4.2 stack_reshape.19
  455.4 5.7 copy.96
  467.0 3.9 reshape.367
  470.9 5.7 copy.98
  485.9 4.8 copy.100
  490.7 4.7 stack_reshape.18
  522.4 76.8 %pmax.7 = f32[1,2,2]{2,1,0:T(2,128)} all-reduce(f32[1,2,2]{2,1,0:T(2,128)S(1)} %get-tuple-element.26), channel_id=1, replica_groups=mesh['rec'=32,'lig'=16] {'rec'}, use_global_device_ids=true, to_apply=%region_12.14 | all-reduce | flops 4 | bytes 32 | tf_op jit(solution)/shard_map/pmax | solution.py:102
  (136 shorter events, 111.5 us)
Async XLA Ops:
  7.2 312.2 %all-reduce.3.cloned.1.call-start = ((), (), s32[]{:S(2)}) async-start(), calls=%async_computation | async-start | bytes 2097152 | tf_op jit(solution)/shard_map/psum | solution.py:11
  67.8 3.8 copy-start.7
  67.8 3.8 copy-start.8
  490.7 6.3 %copy-start = (f32[4,64,1024]{2,1,0:T(8,128)S(1)}, f32[4,64,1024]{2,1,0:T(8,128)}, u32[]{:S(2)}) copy-start(f32[4,64,1024]{2,1,0:T(8,128)} %broadcast_multiply_fusion) | copy-start | bytes 3145732
  499.8 4.1 copy-start.3
  499.8 4.1 copy-start.4
  505.2 4.1 copy-start.1
  505.3 4.1 copy-start.2
  517.6 81.7 %copy-start.5 = (bf16[1,32,1024]{2,1,0:T(8,128)(2,1)S(1)}, bf16[1,32,1024]{2,1,0:T(8,128)(2,1)}, u32[]{:S(2)}) copy-start(bf16[1,32,1024]{2,1,0:T(8,128)(2,1)} %mul.353) | copy-start | bytes 196612
  517.6 81.7 %copy-start.6 = (bf16[1,32,1024]{2,1,0:T(8,128)(2,1)S(1)}, bf16[1,32,1024]{2,1,0:T(8,128)(2,1)}, u32[]{:S(2)}) copy-start(bf16[1,32,1024]{2,1,0:T(8,128)(2,1)} %mul.344) | copy-start | bytes 196612
Sparse Core Ops, SparseCore 0:
  12.1 307.2 all-reduce.2
where the time goes:
time: 619 us; the launch traced here: 607 us
  waiting for transfers between devices  246 us (40%)
  local copies, waits for them, and re-layouts  210 us (34%)
  blocking collectives  96 us (16%)
  matrix products  28.3 us (5%)
  between operations  16.2 us (3%)
  other arithmetic  10.4 us (2%)
    psum x1, waiting for transfers between devices, spread(): return lax.psum(block, axis)  246 us
    reshape x36, local copies, waits for them, and re-layouts, cycle_axes(): shaped = stack.reshape(count, parts, size, size, size)  77.1 us
    pmax x1, blocking collectives, on_device(): best_all = lax.pmax(best, 'rec')  76.8 us
    transpose x10, local copies, waits for them, and re-layouts, cycle_axes(): shaped.transpose(0, 1, 3, 4, 2).reshape(count, parts * size, size * size)  57 us
    reshape x11, local copies, waits for them, and re-layouts, cycle_axes(): shaped.transpose(0, 1, 3, 4, 2).reshape(count, parts * size, size * size)  43.5 us
    dot_general x27, matrix products, apply_rows(): return jnp.einsum('ab,nbm->nam', weight, stack, precision=HIGH)  28.3 us
    all_gather x1, blocking collectives, receptor_spectrum(): whole = lax.all_gather(receptor, 'lig', axis=2, tiled=True)  19.2 us
    another operation x4, local copies, waits for them, and re-layouts, round_spectra(): jnp.stack([forward_full(picked[pose].astype(jnp.float32), cosine, sine) f...  16.7 us
  transfers between devices with their start and end apart: 1, of which 1 were waited for; matrix products, arithmetic and copies ran while one was open for 7% of the time, Pallas kernels for 0%

commit v1 on v0

v1 whole, which is shorter than its diff:
```python
import functools

import jax
import jax.numpy as jnp
import ml_dtypes
import numpy as np
from jax import lax
from jax.experimental import pallas as pl
from jax.experimental.pallas import tpu as pltpu
from jax.sharding import PartitionSpec as P

MESH = pl.DeviceIdType.MESH
G = 32
CELLS = G * G
HALF = G // 2 + 1
LANES = 128
BLOCKS = -(-G * HALF // LANES)
FREQS = BLOCKS * LANES
BF16 = jnp.bfloat16
F32 = jnp.float32


def split_table(table):
    high = table.astype(np.float32).astype(ml_dtypes.bfloat16)
    low = (table - high.astype(np.float64)).astype(np.float32).astype(ml_dtypes.bfloat16)
    return np.stack([high, low], 0)


def plane_tables():
    freq = np.arange(FREQS)
    used = freq < G * HALF
    ky, kz = freq // HALF, freq % HALF
    cell = np.arange(CELLS)
    y, z = cell // G, cell % G
    angle = 2.0 * np.pi * ((y[:, None] * ky + z[:, None] * kz) % G) / G
    cosine = np.where(used, np.cos(angle), 0.0).reshape(CELLS, BLOCKS, LANES)
    sine = np.where(used, np.sin(angle), 0.0).reshape(CELLS, BLOCKS, LANES)
    table = np.stack([cosine, -sine], 2)
    forward = table.transpose(1, 0, 2, 3).reshape(BLOCKS, CELLS, 2 * LANES)
    inverse = forward.transpose(0, 2, 1)
    weight = np.where(used, np.where((kz == 0) | (kz == G // 2), 1.0, 2.0), 0.0)
    return split_table(forward), split_table(inverse), weight.astype(np.float32).reshape(1, FREQS)


def line_table(rows_in, rows_out, sign):
    group_in, x = rows_in
    group_out, k = rows_out
    angle = 2.0 * np.pi * ((k[:, None] * x[None, :]) % G) / G
    same = group_out[:, None] == group_in[None, :]
    cosine = np.where(same, np.cos(angle), 0.0)
    sine = np.where(same, np.sin(angle), 0.0) * sign
    return split_table(np.block([[cosine, sine], [-sine, cosine]]))


def line_tables():
    row = np.arange(128)
    plain = (row // G, row % G)
    lig = ((row // 64) * 2 + (row // 16) % 2, ((row // 32) % 2) * 16 + row % 16)
    rec = ((row // 2) % 4, (row // 8) * 2 + row % 2)
    return np.stack(
        [line_table(lig, plain, 1.0), line_table(rec, plain, 1.0), line_table(plain, plain, -1.0)], 0
    )


def dot(a, b):
    return jnp.dot(a, b, preferred_element_type=F32)


def split(value):
    high = value.astype(BF16)
    return high, (value - high.astype(F32)).astype(BF16)


def line_transform(table, high, low):
    return dot(table[0], high) + dot(table[0], low) + dot(table[1], high)


def kernel(
    n,
    scale,
    own_ref,
    rec_ref,
    weight_ref,
    owners_ref,
    rotations_ref,
    forward_hbm,
    inverse_hbm,
    lines_ref,
    fold_ref,
    scores_ref,
    best_ref,
    best_all_ref,
    forward,
    inverse,
    gathered,
    rec_all,
    plus,
    minus,
    across,
    stage,
    rec_stage,
    rec_spec,
    lig_spec,
    product,
    back,
    total,
    score_v,
    tops,
    table_sem,
    out_sem,
    plus_send,
    plus_recv,
    minus_send,
    minus_recv,
    across_send,
    across_recv,
    gplus_send,
    gplus_recv,
    gminus_send,
    gminus_recv,
    rec_send,
    rec_recv,
    top_send,
    top_recv,
):
    rec = lax.axis_index("rec")
    lig = lax.axis_index("lig")
    ligs = rec_all.shape[0]
    recs = 2 * n
    half = n // 2
    side = rec // n
    me = lax.rem(rec, n)
    right = side * n + lax.rem(me + 1, n)
    left = side * n + lax.rem(me + n - 1, n)
    partner = lax.rem(rec + n, recs)

    tables = [
        pltpu.make_async_copy(forward_hbm, forward, table_sem.at[0]),
        pltpu.make_async_copy(inverse_hbm, inverse, table_sem.at[1]),
    ]
    for copy in tables:
        copy.start()

    barrier = pltpu.get_barrier_semaphore()
    for step in range(1, recs):
        pl.semaphore_signal(
            barrier, inc=1, device_id={"rec": lax.rem(rec + step, recs)}, device_id_type=MESH
        )
    for step in range(1, ligs):
        pl.semaphore_signal(
            barrier, inc=1, device_id={"lig": lax.rem(lig + step, ligs)}, device_id_type=MESH
        )
    rec_all[lig] = rec_ref[...].astype(F32)
    pl.semaphore_wait(barrier, recs + ligs - 2)

    sent = []

    def send(src, dst, send_sem, recv_sem, **where):
        copy = pltpu.make_async_remote_copy(
            src_ref=src,
            dst_ref=dst,
            send_sem=send_sem,
            recv_sem=recv_sem,
            device_id=where,
            device_id_type=MESH,
        )
        copy.start()
        sent.append(copy)
        return copy

    owner = [owners_ref[0, k] for k in range(2)]
    owner_z = [lax.rem(owner[k], n) for k in range(2)]
    mine = [owner_z[k] == me for k in range(2)]

    far = lax.rem(me + half, n)
    copies_p = [[None, None] for _ in range(half)]
    copies_m = [[None, None] for _ in range(half - 1)]
    copies_p[0][0] = send(own_ref.at[far], plus.at[0, 0], plus_send.at[0, 0], plus_recv.at[0, 0], rec=right)
    near = lax.rem(me + n - (half - 1), n)
    copies_m[0][0] = send(own_ref.at[near], minus.at[0, 0], minus_send.at[0, 0], minus_recv.at[0, 0], rec=left)

    gather = []
    for step in range(1, ligs):
        gather.append(
            send(
                rec_all.at[lig],
                rec_all.at[lig],
                rec_send.at[step],
                rec_recv.at[step],
                lig=lax.rem(lig + step, ligs),
            )
        )

    for t in range(1, half):
        for k in range(2):
            slots = [(copies_p, plus, plus_send, plus_recv, lax.rem(me + half - t, n), right)]
            if t < half - 1:
                slots.append(
                    (copies_m, minus, minus_send, minus_recv, lax.rem(me + n - (half - 1) + t, n), left)
                )
            for copies, slot, send_sem, recv_sem, shard, to in slots:
                if t == 1:
                    if k == 0:
                        copies[0][0].wait_recv()
                        seen = slot[0, 0]
                        slot[0, 1] = jnp.where(mine[1], own_ref[shard], seen)
                        slot[0, 0] = jnp.where(mine[0], own_ref[shard], seen)
                else:
                    copies[t - 1][k].wait_recv()
                    slot[t - 1, k] = jnp.where(mine[k], own_ref[shard], slot[t - 1, k])
                copies[t][k] = send(
                    slot.at[t - 1, k], slot.at[t, k], send_sem.at[t, k], recv_sem.at[t, k], rec=to
                )

    crossed = []
    for k in range(2):
        copies_p[half - 1][k].wait_recv()
        copies_m[half - 2][k].wait_recv()
        away = lax.rem(owner_z[k] - me + n, n)
        value = jnp.where(
            away == 0, own_ref[me], jnp.where(away < half, minus[half - 2, k], plus[half - 1, k])
        )
        across[0, k] = value
        crossed.append(
            send(across.at[0, k], across.at[1, k], across_send.at[k], across_recv.at[k], rec=partner)
        )
    gather_p = [[None, None] for _ in range(half)]
    gather_m = [[None, None] for _ in range(half - 1)]
    for k in range(2):
        crossed[k].wait_recv()
        gathered[me, k] = jnp.where(owner[k] // n == side, across[0, k], across[1, k])
        for t in range(1):
            gather_p[t][k] = send(
                gathered.at[me, k], gathered.at[me, k], gplus_send.at[t, k], gplus_recv.at[t, k], rec=right
            )
            gather_m[t][k] = send(
                gathered.at[me, k], gathered.at[me, k], gminus_send.at[t, k], gminus_recv.at[t, k], rec=left
            )
    for t in range(1, half):
        for k in range(2):
            shard = lax.rem(me + n - t, n)
            gather_p[t - 1][k].wait_recv()
            gather_p[t][k] = send(
                gathered.at[shard, k], gathered.at[shard, k], gplus_send.at[t, k], gplus_recv.at[t, k], rec=right
            )
            gather_m[t - 1][k].wait_recv()
            if t < half - 1:
                shard = lax.rem(me + t, n)
                gather_m[t][k] = send(
                    gathered.at[shard, k], gathered.at[shard, k], gminus_send.at[t, k], gminus_recv.at[t, k], rec=left
                )

    for copy in gather:
        copy.wait_recv()
    for copy in tables:
        copy.wait()
    rows = rec_all[...].reshape(128, CELLS).astype(BF16)
    for block in range(BLOCKS):
        lanes = pl.ds(block * LANES, LANES)
        value = dot(rows, forward[0, block]) + dot(rows, forward[1, block])
        for part in range(2):
            high, low = split(value[:, part * LANES : (part + 1) * LANES])
            rec_stage[0, part * 128 : (part + 1) * 128, lanes] = high
            rec_stage[1, part * 128 : (part + 1) * 128, lanes] = low
    rec_spec[...] = line_transform(lines_ref.at[1], rec_stage[0], rec_stage[1]) * fold_ref[...]

    for k in range(2):
        gather_p[half - 1][k].wait_recv()

    @pl.loop(0, 4)
    def _(group):
        data = gathered[pl.ds(group * 4, 4)].reshape(128, CELLS)
        for block in range(BLOCKS):
            lanes = pl.ds(block * LANES, LANES)
            value = dot(data, forward[0, block]) + dot(data, forward[1, block])
            for part in range(2):
                high, low = split(value[:, part * LANES : (part + 1) * LANES])
                stage[0, part * 128 : (part + 1) * 128, lanes] = high
                stage[1, part * 128 : (part + 1) * 128, lanes] = low
        lig_spec[group] = line_transform(lines_ref.at[0], stage[0], stage[1]).astype(BF16).astype(F32)

    for k in range(2):
        for grid in range(2):
            real = imag = None
            for c in range(4):
                weight = weight_ref[c]
                group, row = grid * 2 + c // 2, (c % 2) * 64 + k * 32
                lr = lig_spec[group, row : row + 32]
                li = lig_spec[group, 128 + row : 128 + row + 32]
                rr = rec_spec[c * 32 : c * 32 + 32] * weight
                ri = rec_spec[128 + c * 32 : 128 + c * 32 + 32] * weight
                pr = rr * lr + ri * li
                pi = rr * li - ri * lr
                real = pr if real is None else real + pr
                imag = pi if imag is None else imag + pi
            at = (k * 2 + grid) * 32
            product[at : at + 32] = real
            product[128 + at : 128 + at + 32] = imag

    high, low = split(product[...])
    back[...] = line_transform(lines_ref.at[2], high, low)
    for block in range(BLOCKS):
        lanes = slice(block * LANES, (block + 1) * LANES)
        value = jnp.concatenate([back[:128, lanes], back[128:, lanes]], 1)
        high, low = split(value)
        part = dot(high, inverse[0, block]) + dot(low, inverse[0, block]) + dot(high, inverse[1, block])
        if block == 0:
            total[...] = part
        else:
            total[...] += part

    sub = lax.broadcasted_iota(jnp.int32, (8, LANES), 0)
    top = jnp.zeros((8, LANES), F32)
    for k in range(2):
        first = total[k * 64 : k * 64 + 32] * scale
        second = total[k * 64 + 32 : k * 64 + 64] * scale
        for j in range(2):
            value = jnp.where(rotations_ref[0, k, j] == 0, first, second)
            score_v[k, j] = value.astype(BF16)
            top = jnp.where(sub == k * 2 + j, jnp.max(value), top)
    out = pltpu.make_async_copy(score_v, scores_ref, out_sem)
    out.start()
    tops[rec] = top
    copies = []
    for step in range(1, recs):
        copies.append(
            send(
                tops.at[rec],
                tops.at[rec],
                top_send.at[step],
                top_recv.at[step],
                rec=lax.rem(rec + step, recs),
            )
        )
    best_ref[...] = top
    for copy in copies:
        copy.wait_recv()
    best_all_ref[...] = jnp.max(tops[...], axis=0)
    for copy in sent:
        copy.wait_send()
    out.wait()


def on_device(receptor, ligand_pool, channel_weight, owners, rotations, n, ligs):
    channels = ligand_pool.shape[3]
    scale = 1.0 / (float(G) ** 3 * float(channels * G**3) ** 0.5)
    forward, inverse, fold = plane_tables()
    lines = line_tables()
    own = ligand_pool.reshape(n, 16, CELLS)
    rec = receptor.reshape(8, CELLS)
    half = n // 2
    vmem = pl.BlockSpec(memory_space=pltpu.VMEM)
    smem = pl.BlockSpec(memory_space=pltpu.SMEM)
    hbm = pl.BlockSpec(memory_space=pl.ANY)
    dma = pltpu.SemaphoreType.DMA
    scores, best, best_all = pl.pallas_call(
        functools.partial(kernel, n, scale),
        out_shape=(
            jax.ShapeDtypeStruct((2, 2, G, CELLS), BF16),
            jax.ShapeDtypeStruct((8, LANES), F32),
            jax.ShapeDtypeStruct((8, LANES), F32),
        ),
        in_specs=[vmem, vmem, smem, smem, smem, hbm, hbm, vmem, vmem],
        out_specs=(hbm, vmem, vmem),
        scratch_shapes=[
            pltpu.VMEM(forward.shape, BF16),
            pltpu.VMEM(inverse.shape, BF16),
            pltpu.VMEM((n, 2, 16, CELLS), BF16),
            pltpu.VMEM((ligs, 8, CELLS), F32),
            pltpu.VMEM((half, 2, 16, CELLS), BF16),
            pltpu.VMEM((half - 1, 2, 16, CELLS), BF16),
            pltpu.VMEM((2, 2, 16, CELLS), BF16),
            pltpu.VMEM((2, 256, FREQS), BF16),
            pltpu.VMEM((2, 256, FREQS), BF16),
            pltpu.VMEM((256, FREQS), F32),
            pltpu.VMEM((4, 256, FREQS), F32),
            pltpu.VMEM((256, FREQS), F32),
            pltpu.VMEM((256, FREQS), F32),
            pltpu.VMEM((128, CELLS), F32),
            pltpu.VMEM((2, 2, G, CELLS), BF16),
            pltpu.VMEM((2 * n, 8, LANES), F32),
            dma((2,)),
            dma,
            dma((half, 2)),
            dma((half, 2)),
            dma((half, 2)),
            dma((half, 2)),
            dma((2,)),
            dma((2,)),
            dma((half, 2)),
            dma((half, 2)),
            dma((half, 2)),
            dma((half, 2)),
            dma((ligs,)),
            dma((ligs,)),
            dma((2 * n,)),
            dma((2 * n,)),
        ],
        compiler_params=pltpu.CompilerParams(
            collective_id=0, has_side_effects=True, vmem_limit_bytes=56 * 2**20
        ),
        cost_estimate=pl.CostEstimate(flops=6 * 10**9, bytes_accessed=12 * 2**20, transcendentals=0),
    )(own, rec, channel_weight, owners, rotations, forward, inverse, lines, fold)
    return (
        scores[None, None],
        best[:4, 0].reshape(1, 1, 2, 2),
        best_all[:4, 0].reshape(1, 2, 2),
    )


def solution(mesh):
    in_specs = (
        P("rec", None, "lig", None),
        P("lig", "rec", None, None, None, None),
        P(),
        P("lig", None),
        P("lig", None, None),
    )
    out_specs = (
        P("rec", "lig", None, None, None, None),
        P("rec", "lig", None, None),
        P("lig", None, None),
    )
    body = functools.partial(on_device, n=mesh.shape["rec"] // 2, ligs=mesh.shape["lig"])
    return jax.shard_map(body, mesh=mesh, in_specs=in_specs, out_specs=out_specs, check_vma=False)
```

time: 619 us -> 102 us (0.16); the launches traced: 607 us -> 100 us
  waiting for transfers between devices: 246 us -> 0 us
  local copies, waits for them, and re-layouts: 210 us -> 5.13 us
  blocking collectives: 96 us -> 0 us
  Pallas kernels: 0 us -> 94.7 us
  matrix products: 28.3 us -> 0 us
  between operations: 16.2 us -> 0.64 us
  other arithmetic: 10.4 us -> 0 us
    psum x1 -> x0, waiting for transfers between devices: 246 us -> none  [spread(): return lax.psum(block, axis)]
    reshape x47 -> x1, local copies, waits for them, and re-layouts: 121 us -> 1.34 us  [on_device(): rec = receptor.reshape(8, CELLS)]
    pallas_call x0 -> x1, Pallas kernels: none -> 94.7 us  [on_device(): pl.pallas_call(functools.partial(kernel, n, scale), out_shape=(jax.ShapeD...]
    pmax x1 -> x0, blocking collectives: 76.8 us -> none  [on_device(): best_all = lax.pmax(best, 'rec')]
    transpose x10 -> x0, local copies, waits for them, and re-layouts: 57 us -> none  [cycle_axes(): shaped.transpose(0, 1, 3, 4, 2).reshape(count, parts * size, size * size)]
    dot_general x27 -> x0, matrix products: 28.3 us -> none  [apply_rows(): return jnp.einsum('ab,nbm->nam', weight, stack, precision=HIGH)]
    another operation x12 -> x2, local copies, waits for them, and re-layouts: 20.6 us -> 1.3 us  [the longest x1 0.65 us: on_device(): best[:4, 0].reshape(1, 1, 2, 2)]
    all_gather x1 -> x0, blocking collectives: 19.2 us -> none  [receptor_spectrum(): whole = lax.all_gather(receptor, 'lig', axis=2, tiled=True)]
  transfers between devices with their start and end apart: 1 -> 0, of which waited for: 1 -> 0; matrix products, arithmetic and copies ran while one was open for 7% -> 0% of each run, Pallas kernels for 0% -> 0%
where the time goes in v1:
time: 102 us; the launch traced here: 100 us
  Pallas kernels  94.7 us (93%)
  local copies, waits for them, and re-layouts  5.13 us (5%)
    pallas_call x1, Pallas kernels, on_device(): pl.pallas_call(functools.partial(kernel, n, scale), out_shape=(jax.ShapeD...  94.7 us

profile of v1, /device:TPU:24, one launch (start us, length us, event | category | flops | bytes accessed | tf_op | source)
XLA Modules:
  0.0 100.4 jit_solution(16777588227662296671)
XLA Ops:
  0.6 1.3 %reshape.13.rec_ref = bf16[8,1024]{1,0:T(8,128)(2,1)} reshape(bf16[1,4,2,1024]{3,2,1,0:T(2,128)(2,1)} %param.9) | data formatting | bytes 32768 | tf_op jit(solution)/shard_map/reshape | solution.py:350
  2.0 94.7 %shard_map.112 = (bf16[2,2,32,1024]{3,2,1,0:T(8,128)(2,1)}, f32[8,128]{1,0:T(8,128)}, f32[8,128]{1,0:T(8,128)}) custom-call(bf16[16,16,1024]{2,1,0:T(8,128)(2,1)} %bitcast.3, bf16[8,1024]{1,0:T(8,128)(2,1)} %reshape.13.rec_ref, f32[4]{0:T(128)} %weight_ref.1, s32[1,2]{1,0:T(1,128)} %owners_ref.1, s32[1,2,2]{2,1,0:T(2,128)} %rotations_ref.1, ...), custom_call_target="tpu_custom_call" | custom-call | flops 6000000000 | bytes 12582912 | tf_op jit(solution)/shard_map/pallas_call | solution.py:356
  96.6 0.8 slice_reduce_fusion
  97.5 0.7 reshape_squeeze.6
  98.1 0.6 reshape_squeeze.7
  98.8 1.7 %copy.13 = bf16[1,1,2,2,32,1024]{5,4,3,2,1,0:T(8,128)(2,1)} copy(bf16[1,1,2,2,32,1024]{5,4,3,2,1,0:T(8,128)(2,1)} %bitcast.2) | data formatting | bytes 524288

commit v2 on v1

v2 whole, which is shorter than its diff:
```python
import functools

import jax
import jax.numpy as jnp
import ml_dtypes
import numpy as np
from jax import lax
from jax.experimental import pallas as pl
from jax.experimental.pallas import tpu as pltpu
from jax.sharding import PartitionSpec as P

MESH = pl.DeviceIdType.MESH
G = 32
CELLS = G * G
HALF = G // 2 + 1
LANES = 128
BLOCKS = -(-G * HALF // LANES)
FREQS = BLOCKS * LANES
BF16 = jnp.bfloat16
F32 = jnp.float32


def split_table(table):
    high = table.astype(np.float32).astype(ml_dtypes.bfloat16)
    low = (table - high.astype(np.float64)).astype(np.float32).astype(ml_dtypes.bfloat16)
    return np.stack([high, low], 0)


def plane_tables():
    freq = np.arange(FREQS)
    used = freq < G * HALF
    ky, kz = freq // HALF, freq % HALF
    cell = np.arange(CELLS)
    y, z = cell // G, cell % G
    angle = 2.0 * np.pi * ((y[:, None] * ky + z[:, None] * kz) % G) / G
    cosine = np.where(used, np.cos(angle), 0.0).reshape(CELLS, BLOCKS, LANES)
    sine = np.where(used, np.sin(angle), 0.0).reshape(CELLS, BLOCKS, LANES)
    table = np.stack([cosine, -sine], 2)
    forward = table.transpose(1, 0, 2, 3).reshape(BLOCKS, CELLS, 2 * LANES)
    inverse = forward.transpose(0, 2, 1)
    weight = np.where(used, np.where((kz == 0) | (kz == G // 2), 1.0, 2.0), 0.0)
    return split_table(forward), split_table(inverse), weight.astype(np.float32).reshape(1, FREQS)


def line_table(rows_in, rows_out, sign):
    group_in, x = rows_in
    group_out, k = rows_out
    angle = 2.0 * np.pi * ((k[:, None] * x[None, :]) % G) / G
    same = group_out[:, None] == group_in[None, :]
    cosine = np.where(same, np.cos(angle), 0.0)
    sine = np.where(same, np.sin(angle), 0.0) * sign
    return split_table(np.block([[cosine, sine], [-sine, cosine]]))


def line_tables():
    row = np.arange(128)
    plain = (row // G, row % G)
    lig = ((row // 64) * 2 + (row // 16) % 2, ((row // 32) % 2) * 16 + row % 16)
    rec = ((row // 2) % 4, (row // 8) * 2 + row % 2)
    return np.stack(
        [line_table(lig, plain, 1.0), line_table(rec, plain, 1.0), line_table(plain, plain, -1.0)], 0
    )


def dot(a, b):
    return jnp.dot(a, b, preferred_element_type=F32)


def split(value):
    high = value.astype(BF16)
    return high, (value - high.astype(F32)).astype(BF16)


def line_transform(table, high, low):
    return dot(table[0], high) + dot(table[0], low) + dot(table[1], high)


def plane_transform(rows, forward, block):
    value = None
    for half in range(2):
        for part in range(2):
            term = dot(rows[half], forward[part, block, half * COLS : (half + 1) * COLS])
            value = term if value is None else value + term
    return value


NEAR = (-2, -1, 1, 2)
FAR = (-5, 5)
WINDOW = (-2, -1, 1, 2, 3)
COLS = CELLS // 2


def kernel(
    n,
    scale,
    rec_ref,
    weight_ref,
    owners_ref,
    rotations_ref,
    own_hbm,
    forward_hbm,
    inverse_hbm,
    lines_hbm,
    fold_hbm,
    scores_ref,
    best_ref,
    best_all_ref,
    own,
    forward,
    inverse,
    lines,
    fold,
    leaves,
    ends,
    partial,
    roots,
    gathered,
    rec_all,
    stage,
    rec_stage,
    rec_spec,
    lig_spec,
    product,
    back,
    total,
    score_v,
    tops,
    table_sem,
    out_sem,
    leaf_send,
    leaf_recv,
    end_send,
    end_recv,
    root_send,
    root_recv,
    first_send,
    first_recv,
    relay_send,
    relay_recv,
    last_send,
    last_recv,
    cross_send,
    cross_recv,
    rec_send,
    rec_recv,
    top_send,
    top_recv,
):
    rec = lax.axis_index("rec")
    lig = lax.axis_index("lig")
    side = rec // n
    me = lax.rem(rec, n)
    partner = lax.rem(rec + n, 2 * n)

    def shift(step):
        return lax.rem(me + n + step, n)

    def at(step):
        return side * n + shift(step)

    def over(step):
        return (1 - side) * n + shift(step)

    quad = lig // 4
    quad_peers = [quad * 4 + lax.rem(lig + step, 4) for step in range(1, 4)]
    line_peers = [lax.rem(lig + 4 * step, 16) for step in range(1, 4)]

    barrier = pltpu.get_barrier_semaphore()
    rec_peers = [at(step) for step in (-5, -3, -2, -1, 1, 2, 3, 5)] + [over(step) for step in (-5, 0, 5)]
    for peer in rec_peers:
        pl.semaphore_signal(barrier, inc=1, device_id={"rec": peer}, device_id_type=MESH)
    for peer in quad_peers + line_peers:
        pl.semaphore_signal(barrier, inc=1, device_id={"lig": peer}, device_id_type=MESH)

    loads = [
        pltpu.make_async_copy(src, dst, table_sem.at[i])
        for i, (src, dst) in enumerate(
            [(own_hbm, own), (forward_hbm, forward), (lines_hbm, lines), (fold_hbm, fold), (inverse_hbm, inverse)]
        )
    ]
    for copy in loads:
        copy.start()

    slab = jnp.concatenate([rec_ref[c].astype(F32) for c in range(4)], 0)
    rec_all[lig] = jnp.concatenate([slab[:, :COLS], slab[:, COLS:]], 0).astype(BF16)
    loads[0].wait()
    pl.semaphore_wait(barrier, len(rec_peers) + 6)

    sent = []

    def send(src, dst, send_sem, recv_sem, **where):
        copy = pltpu.make_async_remote_copy(
            src_ref=src,
            dst_ref=dst,
            send_sem=send_sem,
            recv_sem=recv_sem,
            device_id=where,
            device_id_type=MESH,
        )
        copy.start()
        sent.append(copy)
        return copy

    owner = [owners_ref[0, k] for k in range(2)]
    owner_z = [lax.rem(owner[k], n) for k in range(2)]
    owner_side = [owner[k] // n for k in range(2)]

    leaf = {}
    for j, step in ((1, -5), (2, 5), (0, 0)):
        for i, to in enumerate(NEAR):
            leaf[i, j] = send(
                own.at[shift(to + step)], leaves.at[i, j], leaf_send.at[i, j], leaf_recv.at[i, j], rec=at(to)
            )
    far = shift(n // 2)
    end = [
        send(own.at[far, :, :COLS], ends.at[0], end_send.at[0], end_recv.at[0], rec=at(-3)),
        send(own.at[far, :, COLS:], ends.at[1], end_send.at[1], end_recv.at[1], rec=at(3)),
    ]
    slabs = [
        send(rec_all.at[lig], rec_all.at[lig], rec_send.at[0, i], rec_recv.at[0, i], lig=peer)
        for i, peer in enumerate(quad_peers)
    ]
    for copy in slabs:
        copy.wait_recv()
    block = rec_all.at[pl.ds(quad * 4, 4)]
    slabs = [
        send(block, block, rec_send.at[1, i], rec_recv.at[1, i], lig=peer) for i, peer in enumerate(line_peers)
    ]

    root = {}
    for j, step in ((1, -5), (2, 5), (0, 0)):
        shard = shift(step)
        for i in range(len(NEAR)):
            leaf[i, j].wait_recv()
        if j:
            end[j - 1].wait_recv()
        for k in range(2):
            away = lax.rem(owner_z[k] - me + n, n)
            value = own[shard]
            for i, to in enumerate(NEAR):
                value = jnp.where(away == (n - to) % n, leaves[i, j], value)
            parts = [value[:, :COLS], value[:, COLS:]]
            if j == 1:
                parts[0] = jnp.where(away == 3, ends[0], parts[0])
            if j == 2:
                parts[1] = jnp.where(away == n - 3, ends[1], parts[1])
            for half in range(2):
                partial[j, half, k] = parts[half]
        if j:
            for half in range(2):
                slot = (j - 1) * 2 + side
                root[j, half] = send(
                    partial.at[j, half],
                    roots.at[slot],
                    root_send.at[j - 1, half],
                    root_recv.at[slot],
                    rec=half * n + shard,
                )
        else:
            root[0] = send(partial.at[0, 1 - side], roots.at[4], root_send.at[2, 0], root_recv.at[4], rec=partner)

    for copy in slabs:
        copy.wait_recv()
    loads[1].wait()
    loads[2].wait()
    loads[3].wait()
    grid = rec_all[...].astype(F32)
    rows = [grid[:, half * 8 : half * 8 + 8].reshape(128, COLS).astype(BF16) for half in range(2)]
    for block in range(BLOCKS):
        lanes = pl.ds(block * LANES, LANES)
        value = plane_transform(rows, forward, block)
        for part in range(2):
            high, low = split(value[:, part * LANES : (part + 1) * LANES])
            rec_stage[0, part * 128 : (part + 1) * 128, lanes] = high
            rec_stage[1, part * 128 : (part + 1) * 128, lanes] = low
    rec_spec[...] = line_transform(lines.at[1], rec_stage[0], rec_stage[1]) * fold[...]

    def root_wait(slot):
        pltpu.make_async_copy(roots.at[slot], roots.at[slot], root_recv.at[slot]).wait()

    for slot in range(5):
        root_wait(slot)
    for k in range(2):
        away = lax.rem(owner_z[k] - me + n, n)
        below = jnp.logical_or(away > n // 2, jnp.logical_and(away == n // 2, side == 1))
        inner = jnp.logical_or(away <= 2, away >= n - 2)
        here = owner_side[k] == side
        middle = jnp.where(here, partial[0, side, k], roots[4, k])
        up = jnp.where(owner_side[k] == 0, roots[0, k], roots[1, k])
        down = jnp.where(owner_side[k] == 0, roots[2, k], roots[3, k])
        gathered[me, side, k] = jnp.where(inner, middle, jnp.where(below, down, up))

    cross = []

    def spread(shard, lo=0, hi=2):
        ref = gathered.at[shard, side, lo:hi]
        slot = len(cross)
        cross.append(send(ref, ref, cross_send.at[slot], cross_recv.at[slot], rec=partner))

    mine = gathered.at[me, side]
    first = {}
    for i, to in enumerate(FAR + NEAR):
        first[to] = send(mine, mine, first_send.at[i], first_recv.at[i], rec=at(to))
    spread(me)
    relay = {}
    last = []
    for j, to in enumerate(FAR):
        first[to].wait_recv()
        shard = shift(-to)
        ref = gathered.at[shard, side]
        for i, near in enumerate(NEAR):
            relay[i, j] = send(ref, ref, relay_send.at[i, j], relay_recv.at[i, j], rec=at(near))
        ref = gathered.at[shard, side, j]
        last.append(send(ref, ref, last_send.at[j], last_recv.at[j], rec=at(-3 if to < 0 else 3)))
        spread(shard)
    for to in NEAR:
        first[to].wait_recv()
        spread(shift(-to))
    for j, to in enumerate(FAR):
        for i, near in enumerate(NEAR):
            relay[i, j].wait_recv()
            spread(shift(-near - to))
    for j in range(2):
        last[j].wait_recv()
        spread(far, j, j + 1)
    for copy in cross:
        copy.wait_recv()

    @pl.loop(0, 4)
    def _(group):
        data = [gathered[pl.ds(group * 4, 4), half].reshape(128, COLS) for half in range(2)]
        for block in range(BLOCKS):
            lanes = pl.ds(block * LANES, LANES)
            value = plane_transform(data, forward, block)
            for part in range(2):
                high, low = split(value[:, part * LANES : (part + 1) * LANES])
                stage[0, part * 128 : (part + 1) * 128, lanes] = high
                stage[1, part * 128 : (part + 1) * 128, lanes] = low
        lig_spec[group] = line_transform(lines.at[0], stage[0], stage[1]).astype(BF16).astype(F32)

    for k in range(2):
        for grid in range(2):
            real = imag = None
            for c in range(4):
                weight = weight_ref[c]
                group, row = grid * 2 + c // 2, (c % 2) * 64 + k * 32
                lr = lig_spec[group, row : row + 32]
                li = lig_spec[group, 128 + row : 128 + row + 32]
                rr = rec_spec[c * 32 : c * 32 + 32] * weight
                ri = rec_spec[128 + c * 32 : 128 + c * 32 + 32] * weight
                pr = rr * lr + ri * li
                pi = rr * li - ri * lr
                real = pr if real is None else real + pr
                imag = pi if imag is None else imag + pi
            row = (k * 2 + grid) * 32
            product[row : row + 32] = real
            product[128 + row : 128 + row + 32] = imag

    loads[4].wait()
    high, low = split(product[...])
    back[...] = line_transform(lines.at[2], high, low)
    for block in range(BLOCKS):
        lanes = slice(block * LANES, (block + 1) * LANES)
        value = jnp.concatenate([back[:128, lanes], back[128:, lanes]], 1)
        high, low = split(value)
        part = dot(high, inverse[0, block]) + dot(low, inverse[0, block]) + dot(high, inverse[1, block])
        if block == 0:
            total[...] = part
        else:
            total[...] += part

    sub = lax.broadcasted_iota(jnp.int32, (8, LANES), 0)
    lane = lax.broadcasted_iota(jnp.int32, (8, LANES), 1)
    top = jnp.zeros((8, LANES), F32)
    for k in range(2):
        pair = [total[k * 64 : k * 64 + 32] * scale, total[k * 64 + 32 : k * 64 + 64] * scale]
        for j in range(2):
            value = jnp.where(rotations_ref[0, k, j] == 0, pair[0], pair[1])
            score_v[k, j] = value.astype(BF16)
            top = jnp.where(jnp.logical_and(sub == k, lane == j), jnp.max(value), top)
    out = pltpu.make_async_copy(score_v, scores_ref, out_sem)
    out.start()
    best_ref[0, 0] = top[:2, :2]
    tops[0, 5] = top
    copies = [
        send(tops.at[0, 5], tops.at[0, i], top_send.at[0, i], top_recv.at[0, i], rec=at(-step))
        for i, step in enumerate(WINDOW)
    ]
    for copy in copies:
        copy.wait_recv()
    tops[1, 5] = jnp.max(tops[0], axis=0)
    peers = [at(-5), at(5), over(0), over(-5), over(5)]
    copies = [
        send(tops.at[1, 5], tops.at[1, i], top_send.at[1, i], top_recv.at[1, i], rec=peer)
        for i, peer in enumerate(peers)
    ]
    for copy in copies:
        copy.wait_recv()
    best_all_ref[0] = jnp.max(tops[1], axis=0)[:2, :2]
    for copy in sent:
        copy.wait_send()
    out.wait()


def on_device(receptor, ligand_pool, channel_weight, owners, rotations, n, ligs):
    channels = ligand_pool.shape[3]
    scale = 1.0 / (float(G) ** 3 * float(channels * G**3) ** 0.5)
    forward, inverse, fold = plane_tables()
    lines = line_tables()
    own = ligand_pool.reshape(n, 16, CELLS)
    vmem = pl.BlockSpec(memory_space=pltpu.VMEM)
    smem = pl.BlockSpec(memory_space=pltpu.SMEM)
    hbm = pl.BlockSpec(memory_space=pl.ANY)
    dma = pltpu.SemaphoreType.DMA
    scores, best, best_all = pl.pallas_call(
        functools.partial(kernel, n, scale),
        out_shape=(
            jax.ShapeDtypeStruct((2, 2, G, CELLS), BF16),
            jax.ShapeDtypeStruct((1, 1, 2, 2), F32),
            jax.ShapeDtypeStruct((1, 2, 2), F32),
        ),
        in_specs=[vmem, smem, smem, smem, hbm, hbm, hbm, hbm, hbm],
        out_specs=(hbm, vmem, vmem),
        scratch_shapes=[
            pltpu.VMEM((n, 16, CELLS), BF16),
            pltpu.VMEM(forward.shape, BF16),
            pltpu.VMEM(inverse.shape, BF16),
            pltpu.VMEM(lines.shape, BF16),
            pltpu.VMEM(fold.shape, F32),
            pltpu.VMEM((4, 3, 16, CELLS), BF16),
            pltpu.VMEM((2, 16, COLS), BF16),
            pltpu.VMEM((3, 2, 2, 16, COLS), BF16),
            pltpu.VMEM((5, 2, 16, COLS), BF16),
            pltpu.VMEM((n, 2, 2, 16, COLS), BF16),
            pltpu.VMEM((ligs, 16, COLS), BF16),
            pltpu.VMEM((2, 256, FREQS), BF16),
            pltpu.VMEM((2, 256, FREQS), BF16),
            pltpu.VMEM((256, FREQS), F32),
            pltpu.VMEM((4, 256, FREQS), F32),
            pltpu.VMEM((256, FREQS), F32),
            pltpu.VMEM((256, FREQS), F32),
            pltpu.VMEM((128, CELLS), F32),
            pltpu.VMEM((2, 2, G, CELLS), BF16),
            pltpu.VMEM((2, 6, 8, LANES), F32),
            dma((5,)),
            dma,
            dma((4, 3)),
            dma((4, 3)),
            dma((2,)),
            dma((2,)),
            dma((3, 2)),
            dma((5,)),
            dma((6,)),
            dma((6,)),
            dma((4, 2)),
            dma((4, 2)),
            dma((2,)),
            dma((2,)),
            dma((n + 1,)),
            dma((n + 1,)),
            dma((2, 3)),
            dma((2, 3)),
            dma((2, 5)),
            dma((2, 5)),
        ],
        compiler_params=pltpu.CompilerParams(
            collective_id=0, has_side_effects=True, vmem_limit_bytes=56 * 2**20
        ),
        cost_estimate=pl.CostEstimate(flops=6 * 10**9, bytes_accessed=12 * 2**20, transcendentals=0),
    )(receptor[0], channel_weight, owners, rotations, own, forward, inverse, lines, fold)
    return scores[None, None], best, best_all


def solution(mesh):
    in_specs = (
        P("rec", None, "lig", None),
        P("lig", "rec", None, None, None, None),
        P(),
        P("lig", None),
        P("lig", None, None),
    )
    out_specs = (
        P("rec", "lig", None, None, None, None),
        P("rec", "lig", None, None),
        P("lig", None, None),
    )
    body = functools.partial(on_device, n=mesh.shape["rec"] // 2, ligs=mesh.shape["lig"])
    return jax.shard_map(body, mesh=mesh, in_specs=in_specs, out_specs=out_specs, check_vma=False)
```

time: 102 us -> 82.7 us (0.81)
  Pallas kernels: 94.7 us -> 77.1 us
    pallas_call x1, Pallas kernels: 94.7 us -> 77.1 us  [on_device(): pl.pallas_call(functools.partial(kernel, n, scale), out_shape=(jax.ShapeD...]
    unnamed x1 -> x3, local copies, waits for them, and re-layouts: 1.67 us -> 4.13 us
    reshape x1 -> x0, local copies, waits for them, and re-layouts: 1.34 us -> none  [on_device(): rec = receptor.reshape(8, CELLS)]
    another operation x2 -> x0, local copies, waits for them, and re-layouts: 1.3 us -> none  [the longest x1 0.65 us: on_device(): best[:4, 0].reshape(1, 1, 2, 2)]
where the time goes in v2:
time: 82.7 us; the launch traced here: 81.9 us
  Pallas kernels  77.1 us (93%)
  local copies, waits for them, and re-layouts  4.13 us (5%)
    pallas_call x1, Pallas kernels, on_device(): pl.pallas_call(functools.partial(kernel, n, scale), out_shape=(jax.ShapeD...  77.1 us
    unnamed x3, local copies, waits for them, and re-layouts  4.13 us

profile of v2, /device:TPU:24, one launch (start us, length us, event | category | flops | bytes accessed | tf_op | source)
XLA Modules:
  0.0 81.9 jit_solution(1973786207861731120)
XLA Ops:
  0.6 77.1 %shard_map.112 = (bf16[2,2,32,1024]{3,2,1,0:T(8,128)(2,1)}, f32[1,1,2,2]{3,2,1,0:T(2,128)}, f32[1,2,2]{2,1,0:T(2,128)}) custom-call(bf16[4,2,1024]{2,1,0:T(2,128)(2,1)} %bitcast.5, f32[4]{0:T(128)} %weight_ref.1, s32[1,2]{1,0:T(1,128)} %owners_ref.1, s32[1,2,2]{2,1,0:T(2,128)} %rotations_ref.1, bf16[16,16,1024]{2,1,0:T(8,128)(2,1)} %bitcast.4, ...), custom_call_target="tpu_custom_call" | custom-call | flops 6000000000 | bytes 12582912 | tf_op jit(solution)/shard_map/pallas_call | solution.py:415
  77.7 1.7 %copy.15 = bf16[1,1,2,2,32,1024]{5,4,3,2,1,0:T(8,128)(2,1)} copy(bf16[1,1,2,2,32,1024]{5,4,3,2,1,0:T(8,128)(2,1)} %bitcast.3) | data formatting | bytes 524288
  79.4 1.2 %copy.16 = f32[1,1,2,2]{3,2,1,0:T(2,128)} copy(f32[1,1,2,2]{3,2,1,0:T(2,128)} %get-tuple-element.13) | data formatting | bytes 32
  80.6 1.2 %copy.17 = f32[1,2,2]{2,1,0:T(2,128)} copy(f32[1,2,2]{2,1,0:T(2,128)} %get-tuple-element.14) | data formatting | bytes 32

commit v3 on v2

v3 whole, which is shorter than its diff:
```python
import functools

import jax
import jax.numpy as jnp
import ml_dtypes
import numpy as np
from jax import lax
from jax.experimental import pallas as pl
from jax.experimental.pallas import tpu as pltpu
from jax.sharding import PartitionSpec as P

MESH = pl.DeviceIdType.MESH
G = 32
CELLS = G * G
HALF = G // 2 + 1
LANES = 128
BLOCKS = -(-G * HALF // LANES)
FREQS = BLOCKS * LANES
BF16 = jnp.bfloat16
F32 = jnp.float32


def split_table(table):
    high = table.astype(np.float32).astype(ml_dtypes.bfloat16)
    low = (table - high.astype(np.float64)).astype(np.float32).astype(ml_dtypes.bfloat16)
    return np.stack([high, low], 0)


def plane_tables():
    freq = np.arange(FREQS)
    used = freq < G * HALF
    ky, kz = freq // HALF, freq % HALF
    cell = np.arange(CELLS)
    y, z = cell // G, cell % G
    angle = 2.0 * np.pi * ((y[:, None] * ky + z[:, None] * kz) % G) / G
    cosine = np.where(used, np.cos(angle), 0.0).reshape(CELLS, BLOCKS, LANES)
    sine = np.where(used, np.sin(angle), 0.0).reshape(CELLS, BLOCKS, LANES)
    table = np.stack([cosine, -sine], 2)
    forward = table.transpose(1, 0, 2, 3).reshape(BLOCKS, CELLS, 2 * LANES)
    inverse = table.transpose(2, 1, 3, 0).reshape(2 * FREQS, CELLS // 256, 256).transpose(1, 0, 2)
    weight = np.where(used, np.where((kz == 0) | (kz == G // 2), 1.0, 2.0), 0.0)
    return split_table(forward), split_table(inverse), weight.astype(np.float32).reshape(1, FREQS)


def line_table(rows_in, rows_out, sign):
    group_in, x = rows_in
    group_out, k = rows_out
    angle = 2.0 * np.pi * ((k[:, None] * x[None, :]) % G) / G
    same = group_out[:, None] == group_in[None, :]
    cosine = np.where(same, np.cos(angle), 0.0)
    sine = np.where(same, np.sin(angle), 0.0) * sign
    return split_table(np.block([[cosine, sine], [-sine, cosine]]))


def line_tables():
    row = np.arange(128)
    plain = (row // G, row % G)
    rec = ((row // 2) % 4, (row // 8) * 2 + row % 2)
    pair = (plain[0][:64], plain[1][:64])
    forward = np.stack([line_table(plain, plain, 1.0), line_table(rec, plain, 1.0)], 0)
    return forward, line_table(pair, pair, -1.0)


def dot(a, b):
    return jnp.dot(a, b, preferred_element_type=F32)


def split(value):
    high = value.astype(BF16)
    return high, (value - high.astype(F32)).astype(BF16)


def line_transform(table, high, low):
    return dot(table[0], high) + dot(table[0], low) + dot(table[1], high)


def half_plane(data, forward, block, half):
    rows = pl.ds(pl.multiple_of(half * COLS, COLS), COLS)
    return dot(data, forward[0, block, rows]) + dot(data, forward[1, block, rows])


NEAR = (-2, -1, 1, 2)
FAR = (-5, 5)
WINDOW = (-2, -1, 1, 2, 3)
COLS = CELLS // 2


def kernel(
    n,
    scale,
    rec_ref,
    weight_ref,
    owners_ref,
    rotations_ref,
    own_hbm,
    forward_hbm,
    inverse_hbm,
    lines_hbm,
    back_hbm,
    fold_hbm,
    scores_ref,
    tops_ref,
    own,
    forward,
    inverse,
    lines,
    back_lines,
    fold,
    leaves,
    ends,
    partial,
    roots,
    gathered,
    rec_all,
    sums,
    stage,
    rec_stage,
    rec_spec,
    lig_spec,
    product,
    back,
    total,
    score_v,
    tops,
    table_sem,
    out_sem,
    leaf_send,
    leaf_recv,
    end_send,
    end_recv,
    root_send,
    root_recv,
    first_send,
    first_recv,
    relay_send,
    relay_recv,
    last_send,
    last_recv,
    cross_send,
    cross_recv,
    rec_send,
    rec_recv,
    top_send,
    top_recv,
):
    rec = lax.axis_index("rec")
    lig = lax.axis_index("lig")
    side = rec // n
    me = lax.rem(rec, n)
    partner = lax.rem(rec + n, 2 * n)

    def shift(step):
        return lax.rem(me + n + step, n)

    def at(step):
        return side * n + shift(step)

    def over(step):
        return (1 - side) * n + shift(step)

    quad = lig // 4
    quad_peers = [quad * 4 + lax.rem(lig + step, 4) for step in range(1, 4)]
    line_peers = [lax.rem(lig + 4 * step, 16) for step in range(1, 4)]

    barrier = pltpu.get_barrier_semaphore()
    rec_peers = [at(step) for step in (-5, -3, -2, -1, 1, 2, 3, 5)] + [over(step) for step in (-5, 0, 5)]
    for peer in rec_peers:
        pl.semaphore_signal(barrier, inc=1, device_id={"rec": peer}, device_id_type=MESH)
    for peer in quad_peers + line_peers:
        pl.semaphore_signal(barrier, inc=1, device_id={"lig": peer}, device_id_type=MESH)

    loads = [
        pltpu.make_async_copy(src, dst, table_sem.at[i])
        for i, (src, dst) in enumerate(
            [(own_hbm, own), (forward_hbm, forward), (lines_hbm, lines), (fold_hbm, fold), (inverse_hbm, inverse), (back_hbm, back_lines)]
        )
    ]
    for copy in loads:
        copy.start()

    slab = jnp.concatenate([rec_ref[c].astype(F32) for c in range(4)], 0)
    rec_all[lig] = jnp.concatenate([slab[:, :COLS], slab[:, COLS:]], 0).astype(BF16)
    loads[0].wait()
    pl.semaphore_wait(barrier, len(rec_peers) + 6)

    sent = []

    def send(src, dst, send_sem, recv_sem, **where):
        copy = pltpu.make_async_remote_copy(
            src_ref=src,
            dst_ref=dst,
            send_sem=send_sem,
            recv_sem=recv_sem,
            device_id=where,
            device_id_type=MESH,
        )
        copy.start()
        sent.append(copy)
        return copy

    owner = [owners_ref[0, k] for k in range(2)]
    owner_z = [lax.rem(owner[k], n) for k in range(2)]
    owner_side = [owner[k] // n for k in range(2)]

    far = shift(n // 2)
    end = [
        send(own.at[far, :, :COLS], ends.at[0], end_send.at[0], end_recv.at[0], rec=at(-3)),
        send(own.at[far, :, COLS:], ends.at[1], end_send.at[1], end_recv.at[1], rec=at(3)),
    ]
    leaf = {}
    for j, step in ((1, -5), (2, 5), (0, 0)):
        for i, to in enumerate(NEAR):
            leaf[i, j] = send(
                own.at[shift(to + step)], leaves.at[i, j], leaf_send.at[i, j], leaf_recv.at[i, j], rec=at(to)
            )
    slabs = [
        send(rec_all.at[lig], rec_all.at[lig], rec_send.at[0, i], rec_recv.at[0, i], lig=peer)
        for i, peer in enumerate(quad_peers)
    ]
    for copy in slabs:
        copy.wait_recv()
    block = rec_all.at[pl.ds(quad * 4, 4)]
    slabs = [
        send(block, block, rec_send.at[1, i], rec_recv.at[1, i], lig=peer) for i, peer in enumerate(line_peers)
    ]

    root = {}
    for j, step in ((1, -5), (2, 5), (0, 0)):
        shard = shift(step)
        for i in range(len(NEAR)):
            leaf[i, j].wait_recv()
        if j:
            end[j - 1].wait_recv()
        for k in range(2):
            away = lax.rem(owner_z[k] - me + n, n)
            value = own[shard]
            for i, to in enumerate(NEAR):
                value = jnp.where(away == (n - to) % n, leaves[i, j], value)
            parts = [value[:, :COLS], value[:, COLS:]]
            if j == 1:
                parts[0] = jnp.where(away == 3, ends[0], parts[0])
            if j == 2:
                parts[1] = jnp.where(away == n - 3, ends[1], parts[1])
            for half in range(2):
                partial[j, half, k] = parts[half]
            if j:
                for half in range(2):
                    slot = (j - 1) * 2 + side
                    root[j, half, k] = send(
                        partial.at[j, half, k],
                        roots.at[slot, k],
                        root_send.at[j - 1, half, k],
                        root_recv.at[slot, k],
                        rec=half * n + shard,
                    )
            else:
                root[0, k] = send(
                    partial.at[0, 1 - side, k],
                    roots.at[4, k],
                    root_send.at[2, 0, k],
                    root_recv.at[4, k],
                    rec=partner,
                )

    for copy in slabs:
        copy.wait_recv()
    loads[1].wait()
    loads[2].wait()
    loads[3].wait()
    grid = rec_all[...].astype(F32)
    rows = [grid[:, half * 8 : half * 8 + 8].reshape(128, COLS).astype(BF16) for half in range(2)]
    for block in range(BLOCKS):
        lanes = pl.ds(block * LANES, LANES)
        value = half_plane(rows[0], forward, block, 0) + half_plane(rows[1], forward, block, 1)
        for part in range(2):
            high, low = split(value[:, part * LANES : (part + 1) * LANES])
            rec_stage[0, part * 128 : (part + 1) * 128, lanes] = high
            rec_stage[1, part * 128 : (part + 1) * 128, lanes] = low
    rec_spec[...] = line_transform(lines.at[1], rec_stage[0], rec_stage[1]) * fold[...]

    def root_wait(slot, k):
        pltpu.make_async_copy(roots.at[slot, k], roots.at[slot, k], root_recv.at[slot, k]).wait()

    first, relay, last = {}, {}, {}
    cross = [[], []]

    def spread(k, shard):
        ref = gathered.at[k, shard, side]
        slot = len(cross[k])
        cross[k].append(send(ref, ref, cross_send.at[k, slot], cross_recv.at[k, slot], rec=partner))

    def gather_first(k):
        for slot in range(5):
            root_wait(slot, k)
        away = lax.rem(owner_z[k] - me + n, n)
        below = jnp.logical_or(away > n // 2, jnp.logical_and(away == n // 2, side == 1))
        inner = jnp.logical_or(away <= 2, away >= n - 2)
        here = owner_side[k] == side
        middle = jnp.where(here, partial[0, side, k], roots[4, k])
        up = jnp.where(owner_side[k] == 0, roots[0, k], roots[1, k])
        down = jnp.where(owner_side[k] == 0, roots[2, k], roots[3, k])
        gathered[k, me, side] = jnp.where(inner, middle, jnp.where(below, down, up))
        mine = gathered.at[k, me, side]
        for i, to in enumerate(FAR + NEAR):
            first[k, to] = send(mine, mine, first_send.at[i, k], first_recv.at[i, k], rec=at(to))
        spread(k, me)

    def gather_relay(k):
        for j, to in enumerate(FAR):
            first[k, to].wait_recv()
            shard = shift(-to)
            ref = gathered.at[k, shard, side]
            for i, near in enumerate(NEAR):
                relay[i, j, k] = send(ref, ref, relay_send.at[i, j, k], relay_recv.at[i, j, k], rec=at(near))
            if j == k:
                last[k] = send(ref, ref, last_send.at[k], last_recv.at[k], rec=at(-3 if to < 0 else 3))
            spread(k, shard)
        for to in NEAR:
            first[k, to].wait_recv()
            spread(k, shift(-to))

    def gather_cross(k):
        for j, to in enumerate(FAR):
            for i, near in enumerate(NEAR):
                relay[i, j, k].wait_recv()
                spread(k, shift(-near - to))
        last[k].wait_recv()
        spread(k, far)

    for k in range(2):
        gather_first(k)
    for k in range(2):
        gather_relay(k)
    for k in range(2):
        gather_cross(k)

    def half_rows(k, half):
        return gathered[k, :, half].reshape(256, COLS)

    for k in range(2):
        data = half_rows(k, side)
        for block in range(BLOCKS):
            sums[k, block] = half_plane(data, forward, block, side)

    sub = lax.broadcasted_iota(jnp.int32, (8, LANES), 0)
    lane = lax.broadcasted_iota(jnp.int32, (8, LANES), 1)
    top = jnp.zeros((8, LANES), F32)
    for k in range(2):
        for copy in cross[k]:
            copy.wait_recv()

        data = half_rows(k, 1 - side)
        for block in range(BLOCKS):
            lanes = pl.ds(block * LANES, LANES)
            value = sums[k, block] + half_plane(data, forward, block, 1 - side)
            for part in range(2):
                high, low = split(value[:, part * LANES : (part + 1) * LANES])
                for grid in range(2):
                    stage[grid, 0, part * 128 : (part + 1) * 128, lanes] = high[grid * 128 : grid * 128 + 128]
                    stage[grid, 1, part * 128 : (part + 1) * 128, lanes] = low[grid * 128 : grid * 128 + 128]
        for grid in range(2):
            value = line_transform(lines.at[0], stage[grid, 0], stage[grid, 1])
            lig_spec[grid] = value.astype(BF16).astype(F32)

        for grid in range(2):
            real = imag = None
            for c in range(4):
                weight = weight_ref[c]
                lr = lig_spec[grid, c * 32 : c * 32 + 32]
                li = lig_spec[grid, 128 + c * 32 : 128 + c * 32 + 32]
                rr = rec_spec[c * 32 : c * 32 + 32] * weight
                ri = rec_spec[128 + c * 32 : 128 + c * 32 + 32] * weight
                pr = rr * lr + ri * li
                pi = rr * li - ri * lr
                real = pr if real is None else real + pr
                imag = pi if imag is None else imag + pi
            product[grid * 32 : grid * 32 + 32] = real
            product[64 + grid * 32 : 64 + grid * 32 + 32] = imag

        if k == 0:
            loads[4].wait()
            loads[5].wait()
        high, low = split(product[...])
        back[...] = line_transform(back_lines, high, low)
        high, low = split(jnp.concatenate([back[:64], back[64:]], 1))
        both = jnp.concatenate([high, low], 0)
        for tile in range(CELLS // 256):
            part = dot(both, inverse[0, tile])
            total[:, tile * 256 : (tile + 1) * 256] = part[:64] + part[64:] + dot(high, inverse[1, tile])

        pair = [total[:32] * scale, total[32:] * scale]
        for j in range(2):
            value = jnp.where(rotations_ref[0, k, j] == 0, pair[0], pair[1])
            score_v[k, j] = value.astype(BF16)
            top = jnp.where(jnp.logical_and(sub == k, lane == j), jnp.max(value), top)

    out = pltpu.make_async_copy(score_v, scores_ref, out_sem)
    out.start()
    tops_ref[0] = top
    tops[0, 5] = top
    copies = [
        send(tops.at[0, 5], tops.at[0, i], top_send.at[0, i], top_recv.at[0, i], rec=at(-step))
        for i, step in enumerate(WINDOW)
    ]
    for copy in copies:
        copy.wait_recv()
    tops[1, 5] = jnp.max(tops[0], axis=0)
    peers = [at(-5), at(5), over(0), over(-5), over(5)]
    copies = [
        send(tops.at[1, 5], tops.at[1, i], top_send.at[1, i], top_recv.at[1, i], rec=peer)
        for i, peer in enumerate(peers)
    ]
    for copy in copies:
        copy.wait_recv()
    tops_ref[1] = jnp.max(tops[1], axis=0)
    for copy in sent:
        copy.wait_send()
    out.wait()


def write_kernel(scores_in, tops_in, scores_ref, best_ref, best_all_ref, held, in_sem, out_sem):
    reads = [pltpu.make_async_copy(scores_in.at[k], held.at[k], in_sem.at[k]) for k in range(2)]
    writes = [pltpu.make_async_copy(held.at[k], scores_ref.at[k], out_sem.at[k]) for k in range(2)]
    for copy in reads:
        copy.start()
    best_ref[0, 0] = tops_in[0, :2, :2]
    best_all_ref[0] = tops_in[1, :2, :2]
    for k in range(2):
        reads[k].wait()
        writes[k].start()
    for copy in writes:
        copy.wait()


def on_device(receptor, ligand_pool, channel_weight, owners, rotations, n, ligs):
    channels = ligand_pool.shape[3]
    scale = 1.0 / (float(G) ** 3 * float(channels * G**3) ** 0.5)
    forward, inverse, fold = plane_tables()
    lines, back_lines = line_tables()
    own = ligand_pool.reshape(n, 16, CELLS)
    vmem = pl.BlockSpec(memory_space=pltpu.VMEM)
    smem = pl.BlockSpec(memory_space=pltpu.SMEM)
    hbm = pl.BlockSpec(memory_space=pl.ANY)
    dma = pltpu.SemaphoreType.DMA
    scores, tops = pl.pallas_call(
        functools.partial(kernel, n, scale),
        out_shape=(
            jax.ShapeDtypeStruct((2, 2, G, CELLS), BF16),
            jax.ShapeDtypeStruct((2, 8, LANES), F32),
        ),
        in_specs=[vmem, smem, smem, smem, hbm, hbm, hbm, hbm, hbm, hbm],
        out_specs=(hbm, vmem),
        scratch_shapes=[
            pltpu.VMEM((n, 16, CELLS), BF16),
            pltpu.VMEM(forward.shape, BF16),
            pltpu.VMEM(inverse.shape, BF16),
            pltpu.VMEM(lines.shape, BF16),
            pltpu.VMEM(back_lines.shape, BF16),
            pltpu.VMEM(fold.shape, F32),
            pltpu.VMEM((4, 3, 16, CELLS), BF16),
            pltpu.VMEM((2, 16, COLS), BF16),
            pltpu.VMEM((3, 2, 2, 16, COLS), BF16),
            pltpu.VMEM((5, 2, 16, COLS), BF16),
            pltpu.VMEM((2, n, 2, 16, COLS), BF16),
            pltpu.VMEM((ligs, 16, COLS), BF16),
            pltpu.VMEM((2, BLOCKS, 256, 2 * LANES), F32),
            pltpu.VMEM((2, 2, 256, FREQS), BF16),
            pltpu.VMEM((2, 256, FREQS), BF16),
            pltpu.VMEM((256, FREQS), F32),
            pltpu.VMEM((2, 256, FREQS), F32),
            pltpu.VMEM((128, FREQS), F32),
            pltpu.VMEM((128, FREQS), F32),
            pltpu.VMEM((64, CELLS), F32),
            pltpu.VMEM((2, 2, G, CELLS), BF16),
            pltpu.VMEM((2, 6, 8, LANES), F32),
            dma((6,)),
            dma,
            dma((4, 3)),
            dma((4, 3)),
            dma((2,)),
            dma((2,)),
            dma((3, 2, 2)),
            dma((5, 2)),
            dma((6, 2)),
            dma((6, 2)),
            dma((4, 2, 2)),
            dma((4, 2, 2)),
            dma((2,)),
            dma((2,)),
            dma((2, n)),
            dma((2, n)),
            dma((2, 3)),
            dma((2, 3)),
            dma((2, 5)),
            dma((2, 5)),
        ],
        compiler_params=pltpu.CompilerParams(
            collective_id=0, has_side_effects=True, vmem_limit_bytes=56 * 2**20
        ),
        cost_estimate=pl.CostEstimate(flops=6 * 10**9, bytes_accessed=12 * 2**20, transcendentals=0),
    )(receptor[0], channel_weight, owners, rotations, own, forward, inverse, lines, back_lines, fold)
    scores, best, best_all = pl.pallas_call(
        write_kernel,
        out_shape=(
            jax.ShapeDtypeStruct((2, 2, G, CELLS), BF16),
            jax.ShapeDtypeStruct((1, 1, 2, 2), F32),
            jax.ShapeDtypeStruct((1, 2, 2), F32),
        ),
        in_specs=[hbm, vmem],
        out_specs=(hbm, vmem, vmem),
        scratch_shapes=[pltpu.VMEM((2, 2, G, CELLS), BF16), dma((2,)), dma((2,))],
        cost_estimate=pl.CostEstimate(flops=0, bytes_accessed=2**19, transcendentals=0),
    )(scores, tops)
    return scores[None, None], best, best_all


def solution(mesh):
    in_specs = (
        P("rec", None, "lig", None),
        P("lig", "rec", None, None, None, None),
        P(),
        P("lig", None),
        P("lig", None, None),
    )
    out_specs = (
        P("rec", "lig", None, None, None, None),
        P("rec", "lig", None, None),
        P("lig", None, None),
    )
    body = functools.partial(on_device, n=mesh.shape["rec"] // 2, ligs=mesh.shape["lig"])
    return jax.shard_map(body, mesh=mesh, in_specs=in_specs, out_specs=out_specs, check_vma=False)
```

time: 82.7 us -> 73.8 us (0.89)
  Pallas kernels: 77.1 us -> 72.8 us
  local copies, waits for them, and re-layouts: 4.13 us -> 0 us
    pallas_call x1, Pallas kernels: 77.1 us -> 69.9 us  [on_device(): pl.pallas_call(functools.partial(kernel, n, scale), out_shape=(jax.ShapeD...]
    unnamed x3 -> x0, local copies, waits for them, and re-layouts: 4.13 us -> none
    pallas_call x0 -> x1, Pallas kernels: none -> 2.92 us  [on_device(): pl.pallas_call(write_kernel, out_shape=(jax.ShapeDtypeStruct((2, 2, G, CE...]
where the time goes in v3:
time: 73.8 us; the launch traced here: 73.5 us
  Pallas kernels  72.8 us (99%)
    pallas_call x1, Pallas kernels, on_device(): pl.pallas_call(functools.partial(kernel, n, scale), out_shape=(jax.ShapeD...  69.9 us
    pallas_call x1, Pallas kernels, on_device(): pl.pallas_call(write_kernel, out_shape=(jax.ShapeDtypeStruct((2, 2, G, CE...  2.92 us

profile of v3, /device:TPU:24, one launch (start us, length us, event | category | flops | bytes accessed | tf_op | source)
XLA Modules:
  0.0 73.5 jit_solution(6405257202077887686)
XLA Ops:
  0.6 69.9 %shard_map.121 = (bf16[2,2,32,1024]{3,2,1,0:T(8,128)(2,1)}, f32[2,8,128]{2,1,0:T(8,128)}) custom-call(bf16[4,2,1024]{2,1,0:T(2,128)(2,1)} %bitcast.5, f32[4]{0:T(128)} %weight_ref.1, s32[1,2]{1,0:T(1,128)} %owners_ref.1, s32[1,2,2]{2,1,0:T(2,128)} %rotations_ref.1, bf16[16,16,1024]{2,1,0:T(8,128)(2,1)} %bitcast.3, ...), custom_call_target="tpu_custom_call" | custom-call | flops 6000000000 | bytes 12582912 | tf_op jit(solution)/shard_map/pallas_call | solution.py:445
  70.5 2.9 %shard_map.122 = (bf16[2,2,32,1024]{3,2,1,0:T(8,128)(2,1)}, f32[1,1,2,2]{3,2,1,0:T(2,128)}, f32[1,2,2]{2,1,0:T(2,128)}) custom-call(bf16[2,2,32,1024]{3,2,1,0:T(8,128)(2,1)} %get-tuple-element.8.scores_in, f32[2,8,128]{2,1,0:T(8,128)} %get-tuple-element.9.tops_in), custom_call_target="tpu_custom_call" | custom-call | bytes 524288 | tf_op jit(solution)/shard_map/pallas_call | solution.py:502

commit v4 on v3

--- a/solution.py
+++ b/solution.py
@@ -81,7 +81,6 @@
 
 NEAR = (-2, -1, 1, 2)
 FAR = (-5, 5)
-WINDOW = (-2, -1, 1, 2, 3)
 COLS = CELLS // 2
 
 
@@ -163,7 +162,7 @@
     line_peers = [lax.rem(lig + 4 * step, 16) for step in range(1, 4)]
 
     barrier = pltpu.get_barrier_semaphore()
-    rec_peers = [at(step) for step in (-5, -3, -2, -1, 1, 2, 3, 5)] + [over(step) for step in (-5, 0, 5)]
+    rec_peers = [over(step) for step in (-2, 2)] + [at(step) for step in (-3, 3, -2, 2, -1, 1)] + [over(0)]
     for peer in rec_peers:
         pl.semaphore_signal(barrier, inc=1, device_id={"rec": peer}, device_id_type=MESH)
     for peer in quad_peers + line_peers:
@@ -224,13 +223,13 @@
         send(block, block, rec_send.at[1, i], rec_recv.at[1, i], lig=peer) for i, peer in enumerate(line_peers)
     ]
 
+    for copy in end:
+        copy.wait_recv()
     root = {}
     for j, step in ((1, -5), (2, 5), (0, 0)):
         shard = shift(step)
         for i in range(len(NEAR)):
             leaf[i, j].wait_recv()
-        if j:
-            end[j - 1].wait_recv()
         for k in range(2):
             away = lax.rem(owner_z[k] - me + n, n)
             value = own[shard]
@@ -397,22 +396,16 @@
     out = pltpu.make_async_copy(score_v, scores_ref, out_sem)
     out.start()
     tops_ref[0] = top
-    tops[0, 5] = top
+    tops[0] = top
+    steps = sorted(range(1, n), key=lambda step: -min(step, n - step))
+    peers = [over(step) for step in steps[:7]] + [at(step) for step in steps[:7]]
+    peers += [over(step) for step in steps[7:]] + [at(step) for step in steps[7:]] + [over(0)]
     copies = [
-        send(tops.at[0, 5], tops.at[0, i], top_send.at[0, i], top_recv.at[0, i], rec=at(-step))
-        for i, step in enumerate(WINDOW)
+        send(tops.at[0], tops.at[1 + i], top_send.at[i], top_recv.at[i], rec=peer) for i, peer in enumerate(peers)
     ]
     for copy in copies:
         copy.wait_recv()
-    tops[1, 5] = jnp.max(tops[0], axis=0)
-    peers = [at(-5), at(5), over(0), over(-5), over(5)]
-    copies = [
-        send(tops.at[1, 5], tops.at[1, i], top_send.at[1, i], top_recv.at[1, i], rec=peer)
-        for i, peer in enumerate(peers)
-    ]
-    for copy in copies:
-        copy.wait_recv()
-    tops_ref[1] = jnp.max(tops[1], axis=0)
+    tops_ref[1] = jnp.max(tops[...], axis=0)
     for copy in sent:
         copy.wait_send()
     out.wait()
@@ -472,7 +465,7 @@
             pltpu.VMEM((128, FREQS), F32),
             pltpu.VMEM((64, CELLS), F32),
             pltpu.VMEM((2, 2, G, CELLS), BF16),
-            pltpu.VMEM((2, 6, 8, LANES), F32),
+            pltpu.VMEM((2 * n, 8, LANES), F32),
             dma((6,)),
             dma,
             dma((4, 3)),
@@ -491,8 +484,8 @@
             dma((2, n)),
             dma((2, 3)),
             dma((2, 3)),
-            dma((2, 5)),
-            dma((2, 5)),
+            dma((2 * n - 1,)),
+            dma((2 * n - 1,)),
         ],
         compiler_params=pltpu.CompilerParams(
             collective_id=0, has_side_effects=True, vmem_limit_bytes=56 * 2**20

time: 73.8 us -> 70.7 us (0.958)
  Pallas kernels: 72.8 us -> 69.8 us
    pallas_call x1, Pallas kernels: 69.9 us -> 66.8 us  [on_device(): pl.pallas_call(functools.partial(kernel, n, scale), out_shape=(jax.ShapeD...]
where the time goes in v4:
time: 70.7 us; the launch traced here: 70.4 us
  Pallas kernels  69.8 us (99%)
    pallas_call x1, Pallas kernels, on_device(): pl.pallas_call(functools.partial(kernel, n, scale), out_shape=(jax.ShapeD...  66.8 us
    pallas_call x1, Pallas kernels, on_device(): pl.pallas_call(write_kernel, out_shape=(jax.ShapeDtypeStruct((2, 2, G, CE...  2.92 us

profile of v4, /device:TPU:24, one launch (start us, length us, event | category | flops | bytes accessed | tf_op | source)
XLA Modules:
  0.0 70.4 jit_solution(2673523183300030400)
XLA Ops:
  0.6 66.8 %shard_map.121 = (bf16[2,2,32,1024]{3,2,1,0:T(8,128)(2,1)}, f32[2,8,128]{2,1,0:T(8,128)}) custom-call(bf16[4,2,1024]{2,1,0:T(2,128)(2,1)} %bitcast.5, f32[4]{0:T(128)} %weight_ref.1, s32[1,2]{1,0:T(1,128)} %owners_ref.1, s32[1,2,2]{2,1,0:T(2,128)} %rotations_ref.1, bf16[16,16,1024]{2,1,0:T(8,128)(2,1)} %bitcast.3, ...), custom_call_target="tpu_custom_call" | custom-call | flops 6000000000 | bytes 12582912 | tf_op jit(solution)/shard_map/pallas_call | solution.py:438
  67.5 2.9 %shard_map.122 = (bf16[2,2,32,1024]{3,2,1,0:T(8,128)(2,1)}, f32[1,1,2,2]{3,2,1,0:T(2,128)}, f32[1,2,2]{2,1,0:T(2,128)}) custom-call(bf16[2,2,32,1024]{3,2,1,0:T(8,128)(2,1)} %get-tuple-element.8.scores_in, f32[2,8,128]{2,1,0:T(8,128)} %get-tuple-element.9.tops_in), custom_call_target="tpu_custom_call" | custom-call | bytes 524288 | tf_op jit(solution)/shard_map/pallas_call | solution.py:495

commit v5 on v4

--- a/solution.py
+++ b/solution.py
@@ -87,10 +87,10 @@
 def kernel(
     n,
     scale,
-    rec_ref,
-    weight_ref,
-    owners_ref,
-    rotations_ref,
+    rec_hbm,
+    weight_hbm,
+    owners_hbm,
+    rotations_hbm,
     own_hbm,
     forward_hbm,
     inverse_hbm,
@@ -99,6 +99,10 @@
     fold_hbm,
     scores_ref,
     tops_ref,
+    rec_ref,
+    weight_ref,
+    owners_ref,
+    rotations_ref,
     own,
     forward,
     inverse,
@@ -121,6 +125,7 @@
     total,
     score_v,
     tops,
+    small_sem,
     table_sem,
     out_sem,
     leaf_send,
@@ -168,18 +173,28 @@
     for peer in quad_peers + line_peers:
         pl.semaphore_signal(barrier, inc=1, device_id={"lig": peer}, device_id_type=MESH)
 
+    small = [
+        pltpu.make_async_copy(src, dst, small_sem.at[i])
+        for i, (src, dst) in enumerate(
+            [(rec_hbm, rec_ref), (owners_hbm, owners_ref), (rotations_hbm, rotations_ref), (weight_hbm, weight_ref)]
+        )
+    ]
+    small[0].start()
     loads = [
         pltpu.make_async_copy(src, dst, table_sem.at[i])
         for i, (src, dst) in enumerate(
             [(own_hbm, own), (forward_hbm, forward), (lines_hbm, lines), (fold_hbm, fold), (inverse_hbm, inverse), (back_hbm, back_lines)]
         )
     ]
-    for copy in loads:
+    loads[0].start()
+    for copy in small[1:] + loads[1:]:
         copy.start()
+    small[0].wait()
 
     slab = jnp.concatenate([rec_ref[c].astype(F32) for c in range(4)], 0)
     rec_all[lig] = jnp.concatenate([slab[:, :COLS], slab[:, COLS:]], 0).astype(BF16)
-    loads[0].wait()
+    for copy in [loads[0]] + small[1:]:
+        copy.wait()
     pl.semaphore_wait(barrier, len(rec_peers) + 6)
 
     sent = []
@@ -330,13 +345,11 @@
         gather_first(k)
     for k in range(2):
         gather_relay(k)
+    def half_rows(k, half):
+        return gathered[k, :, half].reshape(256, COLS)
+
     for k in range(2):
         gather_cross(k)
-
-    def half_rows(k, half):
-        return gathered[k, :, half].reshape(256, COLS)
-
-    for k in range(2):
         data = half_rows(k, side)
         for block in range(BLOCKS):
             sums[k, block] = half_plane(data, forward, block, side)
@@ -393,9 +406,7 @@
             score_v[k, j] = value.astype(BF16)
             top = jnp.where(jnp.logical_and(sub == k, lane == j), jnp.max(value), top)
 
-    out = pltpu.make_async_copy(score_v, scores_ref, out_sem)
-    out.start()
-    tops_ref[0] = top
+    earlier = list(sent)
     tops[0] = top
     steps = sorted(range(1, n), key=lambda step: -min(step, n - step))
     peers = [over(step) for step in steps[:7]] + [at(step) for step in steps[:7]]
@@ -403,23 +414,34 @@
     copies = [
         send(tops.at[0], tops.at[1 + i], top_send.at[i], top_recv.at[i], rec=peer) for i, peer in enumerate(peers)
     ]
+    out = pltpu.make_async_copy(score_v, scores_ref, out_sem)
+    out.start()
+    tops_ref[0] = top
+    for copy in earlier:
+        copy.wait_send()
+    out.wait()
     for copy in copies:
         copy.wait_recv()
     tops_ref[1] = jnp.max(tops[...], axis=0)
-    for copy in sent:
+    for copy in copies:
         copy.wait_send()
-    out.wait()
-
-
-def write_kernel(scores_in, tops_in, scores_ref, best_ref, best_all_ref, held, in_sem, out_sem):
-    reads = [pltpu.make_async_copy(scores_in.at[k], held.at[k], in_sem.at[k]) for k in range(2)]
+
+
+def write_kernel(scores_in, tops_in, scores_ref, best_ref, best_all_ref, held, tops, best, best_all, in_sem, out_sem):
+    reads = [pltpu.make_async_copy(tops_in, tops, in_sem.at[2])]
+    reads += [pltpu.make_async_copy(scores_in.at[k], held.at[k], in_sem.at[k]) for k in range(2)]
     writes = [pltpu.make_async_copy(held.at[k], scores_ref.at[k], out_sem.at[k]) for k in range(2)]
+    writes.append(pltpu.make_async_copy(best, best_ref, out_sem.at[2]))
+    writes.append(pltpu.make_async_copy(best_all, best_all_ref, out_sem.at[3]))
     for copy in reads:
         copy.start()
-    best_ref[0, 0] = tops_in[0, :2, :2]
-    best_all_ref[0] = tops_in[1, :2, :2]
+    reads[0].wait()
+    best[0, 0] = tops[0, :2, :2]
+    best_all[0] = tops[1, :2, :2]
+    for copy in writes[2:]:
+        copy.start()
     for k in range(2):
-        reads[k].wait()
+        reads[1 + k].wait()
         writes[k].start()
     for copy in writes:
         copy.wait()
@@ -432,7 +454,6 @@
     lines, back_lines = line_tables()
     own = ligand_pool.reshape(n, 16, CELLS)
     vmem = pl.BlockSpec(memory_space=pltpu.VMEM)
-    smem = pl.BlockSpec(memory_space=pltpu.SMEM)
     hbm = pl.BlockSpec(memory_space=pl.ANY)
     dma = pltpu.SemaphoreType.DMA
     scores, tops = pl.pallas_call(
@@ -441,9 +462,13 @@
             jax.ShapeDtypeStruct((2, 2, G, CELLS), BF16),
             jax.ShapeDtypeStruct((2, 8, LANES), F32),
         ),
-        in_specs=[vmem, smem, smem, smem, hbm, hbm, hbm, hbm, hbm, hbm],
+        in_specs=[hbm] * 10,
         out_specs=(hbm, vmem),
         scratch_shapes=[
+            pltpu.VMEM((channels, 2, CELLS), BF16),
+            pltpu.SMEM((channels,), F32),
+            pltpu.SMEM(owners.shape, jnp.int32),
+            pltpu.SMEM(rotations.shape, jnp.int32),
             pltpu.VMEM((n, 16, CELLS), BF16),
             pltpu.VMEM(forward.shape, BF16),
             pltpu.VMEM(inverse.shape, BF16),
@@ -466,6 +491,7 @@
             pltpu.VMEM((64, CELLS), F32),
             pltpu.VMEM((2, 2, G, CELLS), BF16),
             pltpu.VMEM((2 * n, 8, LANES), F32),
+            dma((4,)),
             dma((6,)),
             dma,
             dma((4, 3)),
@@ -499,9 +525,16 @@
             jax.ShapeDtypeStruct((1, 1, 2, 2), F32),
             jax.ShapeDtypeStruct((1, 2, 2), F32),
         ),
-        in_specs=[hbm, vmem],
-        out_specs=(hbm, vmem, vmem),
-        scratch_shapes=[pltpu.VMEM((2, 2, G, CELLS), BF16), dma((2,)), dma((2,))],
+        in_specs=[hbm, hbm],
+        out_specs=(hbm, hbm, hbm),
+        scratch_shapes=[
+            pltpu.VMEM((2, 2, G, CELLS), BF16),
+            pltpu.VMEM((2, 8, LANES), F32),
+            pltpu.VMEM((1, 1, 2, 2), F32),
+            pltpu.VMEM((1, 2, 2), F32),
+            dma((3,)),
+            dma((4,)),
+        ],
         cost_estimate=pl.CostEstimate(flops=0, bytes_accessed=2**19, transcendentals=0),
     )(scores, tops)
     return scores[None, None], best, best_all

time: 70.7 us -> 67.3 us (0.952)
  Pallas kernels: 69.8 us -> 66.5 us
    pallas_call x1, Pallas kernels: 66.8 us -> 64.8 us  [on_device(): pl.pallas_call(functools.partial(kernel, n, scale), out_shape=(jax.ShapeD...]
    pallas_call x1, Pallas kernels: 2.92 us -> 1.7 us  [on_device(): pl.pallas_call(write_kernel, out_shape=(jax.ShapeDtypeStruct((2, 2, G, CE...]
where the time goes in v5:
time: 67.3 us; the launch traced here: 67.1 us
  Pallas kernels  66.5 us (99%)
    pallas_call x1, Pallas kernels, on_device(): pl.pallas_call(functools.partial(kernel, n, scale), out_shape=(jax.ShapeD...  64.8 us
    pallas_call x1, Pallas kernels, on_device(): pl.pallas_call(write_kernel, out_shape=(jax.ShapeDtypeStruct((2, 2, G, CE...  1.7 us

profile of v5, /device:TPU:24, one launch (start us, length us, event | category | flops | bytes accessed | tf_op | source)
XLA Modules:
  0.0 67.1 jit_solution(4460419045226313940)
XLA Ops:
  0.6 64.8 %shard_map.121 = (bf16[2,2,32,1024]{3,2,1,0:T(8,128)(2,1)}, f32[2,8,128]{2,1,0:T(8,128)}) custom-call(bf16[4,2,1024]{2,1,0:T(2,128)(2,1)} %bitcast.5, f32[4]{0:T(128)} %weight_hbm.1, s32[1,2]{1,0:T(1,128)} %owners_hbm.1, s32[1,2,2]{2,1,0:T(2,128)} %rotations_hbm.1, bf16[16,16,1024]{2,1,0:T(8,128)(2,1)} %bitcast.3, ...), custom_call_target="tpu_custom_call" | custom-call | flops 6000000000 | bytes 12582912 | tf_op jit(solution)/shard_map/pallas_call | solution.py:459
  65.4 1.7 %shard_map.122 = (bf16[2,2,32,1024]{3,2,1,0:T(8,128)(2,1)}, f32[1,1,2,2]{3,2,1,0:T(2,128)}, f32[1,2,2]{2,1,0:T(2,128)}) custom-call(bf16[2,2,32,1024]{3,2,1,0:T(8,128)(2,1)} %get-tuple-element.8.scores_in, f32[2,8,128]{2,1,0:T(8,128)} %get-tuple-element.9.tops_in), custom_call_target="tpu_custom_call" | custom-call | bytes 524288 | tf_op jit(solution)/shard_map/pallas_call | solution.py:521

commit v6 on v5

--- a/solution.py
+++ b/solution.py
@@ -12,10 +12,11 @@
 MESH = pl.DeviceIdType.MESH
 G = 32
 CELLS = G * G
-HALF = G // 2 + 1
 LANES = 128
-BLOCKS = -(-G * HALF // LANES)
-FREQS = BLOCKS * LANES
+FREQS = CELLS // 2
+WIDE = FREQS // 2
+BLOCKS = 2
+PACKED = slice(WIDE - LANES, WIDE)
 BF16 = jnp.bfloat16
 F32 = jnp.float32
 
@@ -26,20 +27,42 @@
     return np.stack([high, low], 0)
 
 
+def plane_frequencies():
+    middle = G // 2
+    lists = []
+    for odd in range(2):
+        pairs = [(ky, kz) for kz in range(1, middle) for ky in range(odd, G, 2)]
+        pairs += [(ky, kz) for kz in (0, middle) for ky in range(odd, middle, 2) if ky]
+        lists.append(pairs)
+    first = lists[0] + [(0, 0), (0, middle)] + lists[1]
+    second = lists[0] + [(middle, 0), (middle, middle)] + lists[1]
+    return np.array(first), np.array(second)
+
+
 def plane_tables():
-    freq = np.arange(FREQS)
-    used = freq < G * HALF
-    ky, kz = freq // HALF, freq % HALF
+    first, second = plane_frequencies()
     cell = np.arange(CELLS)
     y, z = cell // G, cell % G
-    angle = 2.0 * np.pi * ((y[:, None] * ky + z[:, None] * kz) % G) / G
-    cosine = np.where(used, np.cos(angle), 0.0).reshape(CELLS, BLOCKS, LANES)
-    sine = np.where(used, np.sin(angle), 0.0).reshape(CELLS, BLOCKS, LANES)
-    table = np.stack([cosine, -sine], 2)
-    forward = table.transpose(1, 0, 2, 3).reshape(BLOCKS, CELLS, 2 * LANES)
-    inverse = table.transpose(2, 1, 3, 0).reshape(2 * FREQS, CELLS // 256, 256).transpose(1, 0, 2)
-    weight = np.where(used, np.where((kz == 0) | (kz == G // 2), 1.0, 2.0), 0.0)
+
+    def angle(pairs):
+        return 2.0 * np.pi * ((y[:, None] * pairs[:, 0] + z[:, None] * pairs[:, 1]) % G) / G
+
+    paired = np.any(first != second, axis=1)
+    real = np.cos(angle(first))
+    imag = np.where(paired, np.cos(angle(second)), -np.sin(angle(first)))
+    table = np.stack([real.reshape(CELLS, BLOCKS, WIDE), imag.reshape(CELLS, BLOCKS, WIDE)], 2)
+    forward = table.transpose(1, 0, 2, 3).reshape(BLOCKS, CELLS, 2 * WIDE)
+    inverse = forward[:, : CELLS // 2].transpose(0, 2, 1)
+    weight = np.where(paired, 1.0, 2.0)
     return split_table(forward), split_table(inverse), weight.astype(np.float32).reshape(1, FREQS)
+
+
+def mirror_table():
+    row = np.arange(256)
+    source = row // G * G + (G - row % G) % G
+    table = np.zeros((256, 256))
+    table[row, source] = np.where(row < 128, 1.0, -1.0)
+    return table.astype(ml_dtypes.bfloat16)
 
 
 def line_table(rows_in, rows_out, sign):
@@ -96,6 +119,7 @@
     inverse_hbm,
     lines_hbm,
     back_hbm,
+    mirror_hbm,
     fold_hbm,
     scores_ref,
     tops_ref,
@@ -108,6 +132,7 @@
     inverse,
     lines,
     back_lines,
+    mirror,
     fold,
     leaves,
     ends,
@@ -119,7 +144,9 @@
     stage,
     rec_stage,
     rec_spec,
+    rec_cross,
     lig_spec,
+    lig_cross,
     product,
     back,
     total,
@@ -183,7 +210,7 @@
     loads = [
         pltpu.make_async_copy(src, dst, table_sem.at[i])
         for i, (src, dst) in enumerate(
-            [(own_hbm, own), (forward_hbm, forward), (lines_hbm, lines), (fold_hbm, fold), (inverse_hbm, inverse), (back_hbm, back_lines)]
+            [(own_hbm, own), (forward_hbm, forward), (lines_hbm, lines), (fold_hbm, fold), (inverse_hbm, inverse), (back_hbm, back_lines), (mirror_hbm, mirror)]
         )
     ]
     loads[0].start()
@@ -283,14 +310,28 @@
     loads[3].wait()
     grid = rec_all[...].astype(F32)
     rows = [grid[:, half * 8 : half * 8 + 8].reshape(128, COLS).astype(BF16) for half in range(2)]
+    loads[6].wait()
     for block in range(BLOCKS):
-        lanes = pl.ds(block * LANES, LANES)
+        lanes = pl.ds(block * WIDE, WIDE)
         value = half_plane(rows[0], forward, block, 0) + half_plane(rows[1], forward, block, 1)
         for part in range(2):
-            high, low = split(value[:, part * LANES : (part + 1) * LANES])
+            high, low = split(value[:, part * WIDE : (part + 1) * WIDE])
             rec_stage[0, part * 128 : (part + 1) * 128, lanes] = high
             rec_stage[1, part * 128 : (part + 1) * 128, lanes] = low
-    rec_spec[...] = line_transform(lines.at[1], rec_stage[0], rec_stage[1]) * fold[...]
+    value = line_transform(lines.at[1], rec_stage[0], rec_stage[1]) * fold[...]
+    for c in range(4):
+        for part in range(2):
+            at_row = slice(part * 128 + c * 32, part * 128 + c * 32 + 32)
+            rec_spec[at_row] = value[at_row] * weight_ref[c]
+    value = rec_spec[:, PACKED]
+    high, low = split(value)
+    turned = dot(mirror[...], high) + dot(mirror[...], low)
+    a, b, c, d = value[:128], value[128:], turned[:128], turned[128:]
+    pair = lax.broadcasted_iota(jnp.int32, (128, LANES), 1) >= LANES - 2
+    rec_spec[:128, PACKED] = jnp.where(pair, (a + b + c - d) * 0.25, a)
+    rec_spec[128:, PACKED] = jnp.where(pair, (b - a + c + d) * 0.25, b)
+    rec_cross[:128] = jnp.where(pair, (a - b + c + d) * 0.25, 0.0)
+    rec_cross[128:] = jnp.where(pair, (a + b + d - c) * 0.25, 0.0)
 
     def root_wait(slot, k):
         pltpu.make_async_copy(roots.at[slot, k], roots.at[slot, k], root_recv.at[slot, k]).wait()
@@ -363,42 +404,44 @@
 
         data = half_rows(k, 1 - side)
         for block in range(BLOCKS):
-            lanes = pl.ds(block * LANES, LANES)
+            lanes = pl.ds(block * WIDE, WIDE)
             value = sums[k, block] + half_plane(data, forward, block, 1 - side)
             for part in range(2):
-                high, low = split(value[:, part * LANES : (part + 1) * LANES])
+                high, low = split(value[:, part * WIDE : (part + 1) * WIDE])
                 for grid in range(2):
                     stage[grid, 0, part * 128 : (part + 1) * 128, lanes] = high[grid * 128 : grid * 128 + 128]
                     stage[grid, 1, part * 128 : (part + 1) * 128, lanes] = low[grid * 128 : grid * 128 + 128]
+
         for grid in range(2):
-            value = line_transform(lines.at[0], stage[grid, 0], stage[grid, 1])
-            lig_spec[grid] = value.astype(BF16).astype(F32)
-
-        for grid in range(2):
-            real = imag = None
+            value = line_transform(lines.at[0], stage[grid, 0], stage[grid, 1]).astype(BF16)
+            lig_spec[...] = value.astype(F32)
+            lig_cross[...] = dot(mirror[...], value[:, PACKED])
+            real = imag = 0.0
+            real_cross = imag_cross = 0.0
             for c in range(4):
-                weight = weight_ref[c]
-                lr = lig_spec[grid, c * 32 : c * 32 + 32]
-                li = lig_spec[grid, 128 + c * 32 : 128 + c * 32 + 32]
-                rr = rec_spec[c * 32 : c * 32 + 32] * weight
-                ri = rec_spec[128 + c * 32 : 128 + c * 32 + 32] * weight
-                pr = rr * lr + ri * li
-                pi = rr * li - ri * lr
-                real = pr if real is None else real + pr
-                imag = pi if imag is None else imag + pi
-            product[grid * 32 : grid * 32 + 32] = real
-            product[64 + grid * 32 : 64 + grid * 32 + 32] = imag
+                re, im = slice(c * 32, c * 32 + 32), slice(128 + c * 32, 128 + c * 32 + 32)
+                real += rec_spec[re] * lig_spec[re] + rec_spec[im] * lig_spec[im]
+                imag += rec_spec[re] * lig_spec[im] - rec_spec[im] * lig_spec[re]
+                real_cross += rec_cross[re] * lig_cross[re] + rec_cross[im] * lig_cross[im]
+                imag_cross += rec_cross[re] * lig_cross[im] - rec_cross[im] * lig_cross[re]
+            for part, whole, crossed in ((0, real, real_cross), (64, imag, imag_cross)):
+                at_row = slice(part + grid * 32, part + grid * 32 + 32)
+                product[at_row] = whole
+                product[at_row, PACKED] = whole[:, PACKED] + crossed
 
         if k == 0:
             loads[4].wait()
             loads[5].wait()
         high, low = split(product[...])
         back[...] = line_transform(back_lines, high, low)
-        high, low = split(jnp.concatenate([back[:64], back[64:]], 1))
-        both = jnp.concatenate([high, low], 0)
-        for tile in range(CELLS // 256):
-            part = dot(both, inverse[0, tile])
-            total[:, tile * 256 : (tile + 1) * 256] = part[:64] + part[64:] + dot(high, inverse[1, tile])
+        folded = []
+        for block in range(BLOCKS):
+            lanes = slice(block * WIDE, (block + 1) * WIDE)
+            high, low = split(jnp.concatenate([back[:64, lanes], back[64:, lanes]], 1))
+            part = dot(jnp.concatenate([high, low], 0), inverse[0, block])
+            folded.append(part[:64] + part[64:] + dot(high, inverse[1, block]))
+        total[:, : CELLS // 2] = folded[0] + folded[1]
+        total[:, CELLS // 2 :] = folded[0] - folded[1]
 
         pair = [total[:32] * scale, total[32:] * scale]
         for j in range(2):
@@ -452,6 +495,7 @@
     scale = 1.0 / (float(G) ** 3 * float(channels * G**3) ** 0.5)
     forward, inverse, fold = plane_tables()
     lines, back_lines = line_tables()
+    mirror = mirror_table()
     own = ligand_pool.reshape(n, 16, CELLS)
     vmem = pl.BlockSpec(memory_space=pltpu.VMEM)
     hbm = pl.BlockSpec(memory_space=pl.ANY)
@@ -462,7 +506,7 @@
             jax.ShapeDtypeStruct((2, 2, G, CELLS), BF16),
             jax.ShapeDtypeStruct((2, 8, LANES), F32),
         ),
-        in_specs=[hbm] * 10,
+        in_specs=[hbm] * 11,
         out_specs=(hbm, vmem),
         scratch_shapes=[
             pltpu.VMEM((channels, 2, CELLS), BF16),
@@ -474,6 +518,7 @@
             pltpu.VMEM(inverse.shape, BF16),
             pltpu.VMEM(lines.shape, BF16),
             pltpu.VMEM(back_lines.shape, BF16),
+            pltpu.VMEM(mirror.shape, BF16),
             pltpu.VMEM(fold.shape, F32),
             pltpu.VMEM((4, 3, 16, CELLS), BF16),
             pltpu.VMEM((2, 16, COLS), BF16),
@@ -481,18 +526,20 @@
             pltpu.VMEM((5, 2, 16, COLS), BF16),
             pltpu.VMEM((2, n, 2, 16, COLS), BF16),
             pltpu.VMEM((ligs, 16, COLS), BF16),
-            pltpu.VMEM((2, BLOCKS, 256, 2 * LANES), F32),
+            pltpu.VMEM((2, BLOCKS, 256, 2 * WIDE), F32),
             pltpu.VMEM((2, 2, 256, FREQS), BF16),
             pltpu.VMEM((2, 256, FREQS), BF16),
             pltpu.VMEM((256, FREQS), F32),
-            pltpu.VMEM((2, 256, FREQS), F32),
+            pltpu.VMEM((256, LANES), F32),
+            pltpu.VMEM((256, FREQS), F32),
+            pltpu.VMEM((256, LANES), F32),
             pltpu.VMEM((128, FREQS), F32),
             pltpu.VMEM((128, FREQS), F32),
             pltpu.VMEM((64, CELLS), F32),
             pltpu.VMEM((2, 2, G, CELLS), BF16),
             pltpu.VMEM((2 * n, 8, LANES), F32),
             dma((4,)),
-            dma((6,)),
+            dma((7,)),
             dma,
             dma((4, 3)),
             dma((4, 3)),
@@ -517,7 +564,7 @@
             collective_id=0, has_side_effects=True, vmem_limit_bytes=56 * 2**20
         ),
         cost_estimate=pl.CostEstimate(flops=6 * 10**9, bytes_accessed=12 * 2**20, transcendentals=0),
-    )(receptor[0], channel_weight, owners, rotations, own, forward, inverse, lines, back_lines, fold)
+    )(receptor[0], channel_weight, owners, rotations, own, forward, inverse, lines, back_lines, mirror, fold)
     scores, best, best_all = pl.pallas_call(
         write_kernel,
         out_shape=(

time: 67.3 us -> 65.7 us (0.976)
  Pallas kernels: 66.5 us -> 64.9 us
    pallas_call x1, Pallas kernels: 64.8 us -> 63.2 us  [on_device(): pl.pallas_call(functools.partial(kernel, n, scale), out_shape=(jax.ShapeD...]
where the time goes in v6:
time: 65.7 us; the launch traced here: 65.6 us
  Pallas kernels  64.9 us (99%)
    pallas_call x1, Pallas kernels, on_device(): pl.pallas_call(functools.partial(kernel, n, scale), out_shape=(jax.ShapeD...  63.2 us
    pallas_call x1, Pallas kernels, on_device(): pl.pallas_call(write_kernel, out_shape=(jax.ShapeDtypeStruct((2, 2, G, CE...  1.7 us

profile of v6, /device:TPU:24, one launch (start us, length us, event | category | flops | bytes accessed | tf_op | source)
XLA Modules:
  0.0 65.6 jit_solution(9399703541006869481)
XLA Ops:
  0.6 63.2 %shard_map.130 = (bf16[2,2,32,1024]{3,2,1,0:T(8,128)(2,1)}, f32[2,8,128]{2,1,0:T(8,128)}) custom-call(bf16[4,2,1024]{2,1,0:T(2,128)(2,1)} %bitcast.5, f32[4]{0:T(128)} %weight_hbm.1, s32[1,2]{1,0:T(1,128)} %owners_hbm.1, s32[1,2,2]{2,1,0:T(2,128)} %rotations_hbm.1, bf16[16,16,1024]{2,1,0:T(8,128)(2,1)} %bitcast.3, ...), custom_call_target="tpu_custom_call" | custom-call | flops 6000000000 | bytes 12582912 | tf_op jit(solution)/shard_map/pallas_call | solution.py:503
  63.9 1.7 %shard_map.131 = (bf16[2,2,32,1024]{3,2,1,0:T(8,128)(2,1)}, f32[1,1,2,2]{3,2,1,0:T(2,128)}, f32[1,2,2]{2,1,0:T(2,128)}) custom-call(bf16[2,2,32,1024]{3,2,1,0:T(8,128)(2,1)} %get-tuple-element.8.scores_in, f32[2,8,128]{2,1,0:T(8,128)} %get-tuple-element.9.tops_in), custom_call_target="tpu_custom_call" | custom-call | bytes 524288 | tf_op jit(solution)/shard_map/pallas_call | solution.py:568

commit v7 on v6

--- a/solution.py
+++ b/solution.py
@@ -152,6 +152,7 @@
     total,
     score_v,
     tops,
+    known_sem,
     small_sem,
     table_sem,
     out_sem,
@@ -194,7 +195,7 @@
     line_peers = [lax.rem(lig + 4 * step, 16) for step in range(1, 4)]
 
     barrier = pltpu.get_barrier_semaphore()
-    rec_peers = [over(step) for step in (-2, 2)] + [at(step) for step in (-3, 3, -2, 2, -1, 1)] + [over(0)]
+    rec_peers = [at(step) for step in (-3, 3, -2, 2)] + [over(0), at(-1), at(1)]
     for peer in rec_peers:
         pl.semaphore_signal(barrier, inc=1, device_id={"rec": peer}, device_id_type=MESH)
     for peer in quad_peers + line_peers:
@@ -267,11 +268,15 @@
 
     for copy in end:
         copy.wait_recv()
+    for step in (-2, 2):
+        pl.semaphore_signal(known_sem, inc=1, device_id={"rec": at(step)}, device_id_type=MESH)
     root = {}
     for j, step in ((1, -5), (2, 5), (0, 0)):
         shard = shift(step)
         for i in range(len(NEAR)):
             leaf[i, j].wait_recv()
+        if j == 1:
+            pl.semaphore_wait(known_sem, 2)
         for k in range(2):
             away = lax.rem(owner_z[k] - me + n, n)
             value = own[shard]
@@ -339,10 +344,17 @@
     first, relay, last = {}, {}, {}
     cross = [[], []]
 
-    def spread(k, shard):
-        ref = gathered.at[k, shard, side]
+    def spread(k, lo, hi):
         slot = len(cross[k])
-        cross[k].append(send(ref, ref, cross_send.at[k, slot], cross_recv.at[k, slot], rec=partner))
+        cross[k].append(
+            send(
+                gathered.at[k, 0, lo:hi],
+                gathered.at[k, 1, lo:hi],
+                cross_send.at[k, slot],
+                cross_recv.at[k, slot],
+                rec=partner,
+            )
+        )
 
     def gather_first(k):
         for slot in range(5):
@@ -354,44 +366,53 @@
         middle = jnp.where(here, partial[0, side, k], roots[4, k])
         up = jnp.where(owner_side[k] == 0, roots[0, k], roots[1, k])
         down = jnp.where(owner_side[k] == 0, roots[2, k], roots[3, k])
-        gathered[k, me, side] = jnp.where(inner, middle, jnp.where(below, down, up))
-        mine = gathered.at[k, me, side]
+        gathered[k, 0, 8] = jnp.where(inner, middle, jnp.where(below, down, up))
         for i, to in enumerate(FAR + NEAR):
-            first[k, to] = send(mine, mine, first_send.at[i, k], first_recv.at[i, k], rec=at(to))
-        spread(k, me)
+            first[k, to] = send(
+                gathered.at[k, 0, 8],
+                gathered.at[k, 0, 8 - to],
+                first_send.at[i, k],
+                first_recv.at[i, k],
+                rec=at(to),
+            )
 
     def gather_relay(k):
         for j, to in enumerate(FAR):
             first[k, to].wait_recv()
-            shard = shift(-to)
-            ref = gathered.at[k, shard, side]
+            ref = gathered.at[k, 0, 8 - to]
             for i, near in enumerate(NEAR):
-                relay[i, j, k] = send(ref, ref, relay_send.at[i, j, k], relay_recv.at[i, j, k], rec=at(near))
+                relay[i, j, k] = send(
+                    ref, gathered.at[k, 0, 8 - to - near], relay_send.at[i, j, k], relay_recv.at[i, j, k], rec=at(near)
+                )
             if j == k:
-                last[k] = send(ref, ref, last_send.at[k], last_recv.at[k], rec=at(-3 if to < 0 else 3))
-            spread(k, shard)
+                last[k] = send(
+                    ref, gathered.at[k, 0, 0], last_send.at[k], last_recv.at[k], rec=at(-3 if to < 0 else 3)
+                )
+            spread(k, 8 - to, 9 - to)
         for to in NEAR:
             first[k, to].wait_recv()
-            spread(k, shift(-to))
+        spread(k, 6, 11)
 
     def gather_cross(k):
         for j, to in enumerate(FAR):
-            for i, near in enumerate(NEAR):
-                relay[i, j, k].wait_recv()
-                spread(k, shift(-near - to))
+            for pair in ((0, 1), (2, 3)):
+                for i in pair:
+                    relay[i, j, k].wait_recv()
+                lo = 8 - to - max(NEAR[i] for i in pair)
+                spread(k, lo, lo + 2)
         last[k].wait_recv()
-        spread(k, far)
+        spread(k, 0, 1)
 
     for k in range(2):
         gather_first(k)
     for k in range(2):
         gather_relay(k)
-    def half_rows(k, half):
-        return gathered[k, :, half].reshape(256, COLS)
+    def half_rows(k, line):
+        return jnp.concatenate([gathered[k, line, lax.rem(s + n + 8 - me, n)] for s in range(n)], 0)
 
     for k in range(2):
         gather_cross(k)
-        data = half_rows(k, side)
+        data = half_rows(k, 0)
         for block in range(BLOCKS):
             sums[k, block] = half_plane(data, forward, block, side)
 
@@ -402,7 +423,7 @@
         for copy in cross[k]:
             copy.wait_recv()
 
-        data = half_rows(k, 1 - side)
+        data = half_rows(k, 1)
         for block in range(BLOCKS):
             lanes = pl.ds(block * WIDE, WIDE)
             value = sums[k, block] + half_plane(data, forward, block, 1 - side)
@@ -443,20 +464,29 @@
         total[:, : CELLS // 2] = folded[0] + folded[1]
         total[:, CELLS // 2 :] = folded[0] - folded[1]
 
-        pair = [total[:32] * scale, total[32:] * scale]
+        def store_scores(k):
+            for j in range(2):
+                value = jnp.where(rotations_ref[0, k, j] == 0, total[:32], total[32:])
+                score_v[k, j] = (value * scale).astype(BF16)
+
+        tall = [jnp.max(total[:32]) * scale, jnp.max(total[32:]) * scale]
         for j in range(2):
-            value = jnp.where(rotations_ref[0, k, j] == 0, pair[0], pair[1])
-            score_v[k, j] = value.astype(BF16)
-            top = jnp.where(jnp.logical_and(sub == k, lane == j), jnp.max(value), top)
+            value = jnp.where(rotations_ref[0, k, j] == 0, tall[0], tall[1])
+            top = jnp.where(jnp.logical_and(sub == k, lane == j), value, top)
+        if k == 0:
+            store_scores(0)
 
     earlier = list(sent)
     tops[0] = top
+    two = pl.ds(0, 2)
     steps = sorted(range(1, n), key=lambda step: -min(step, n - step))
     peers = [over(step) for step in steps[:7]] + [at(step) for step in steps[:7]]
     peers += [over(step) for step in steps[7:]] + [at(step) for step in steps[7:]] + [over(0)]
     copies = [
-        send(tops.at[0], tops.at[1 + i], top_send.at[i], top_recv.at[i], rec=peer) for i, peer in enumerate(peers)
+        send(tops.at[0, two], tops.at[1 + i, two], top_send.at[i], top_recv.at[i], rec=peer)
+        for i, peer in enumerate(peers)
     ]
+    store_scores(1)
     out = pltpu.make_async_copy(score_v, scores_ref, out_sem)
     out.start()
     tops_ref[0] = top
@@ -465,7 +495,7 @@
     out.wait()
     for copy in copies:
         copy.wait_recv()
-    tops_ref[1] = jnp.max(tops[...], axis=0)
+    tops_ref[1, :2] = jnp.max(tops[:, :2], axis=0)
     for copy in copies:
         copy.wait_send()
 
@@ -524,7 +554,7 @@
             pltpu.VMEM((2, 16, COLS), BF16),
             pltpu.VMEM((3, 2, 2, 16, COLS), BF16),
             pltpu.VMEM((5, 2, 16, COLS), BF16),
-            pltpu.VMEM((2, n, 2, 16, COLS), BF16),
+            pltpu.VMEM((2, 2, n, 16, COLS), BF16),
             pltpu.VMEM((ligs, 16, COLS), BF16),
             pltpu.VMEM((2, BLOCKS, 256, 2 * WIDE), F32),
             pltpu.VMEM((2, 2, 256, FREQS), BF16),
@@ -538,6 +568,7 @@
             pltpu.VMEM((64, CELLS), F32),
             pltpu.VMEM((2, 2, G, CELLS), BF16),
             pltpu.VMEM((2 * n, 8, LANES), F32),
+            pltpu.SemaphoreType.REGULAR,
             dma((4,)),
             dma((7,)),
             dma,
@@ -553,8 +584,8 @@
             dma((4, 2, 2)),
             dma((2,)),
             dma((2,)),
-            dma((2, n)),
-            dma((2, n)),
+            dma((2, 8)),
+            dma((2, 8)),
             dma((2, 3)),
             dma((2, 3)),
             dma((2 * n - 1,)),

time: 65.7 us -> 64.4 us (0.980)
  Pallas kernels: 64.9 us -> 63.6 us
    pallas_call x1, Pallas kernels: 63.2 us -> 61.9 us  [on_device(): pl.pallas_call(functools.partial(kernel, n, scale), out_shape=(jax.ShapeD...]
where the time goes in v7:
time: 64.4 us; the launch traced here: 64.2 us
  Pallas kernels  63.6 us (99%)
    pallas_call x1, Pallas kernels, on_device(): pl.pallas_call(functools.partial(kernel, n, scale), out_shape=(jax.ShapeD...  61.9 us
    pallas_call x1, Pallas kernels, on_device(): pl.pallas_call(write_kernel, out_shape=(jax.ShapeDtypeStruct((2, 2, G, CE...  1.7 us

profile of v7, /device:TPU:24, one launch (start us, length us, event | category | flops | bytes accessed | tf_op | source)
XLA Modules:
  0.0 64.2 jit_solution(11938947576933023105)
XLA Ops:
  0.6 61.9 %shard_map.130 = (bf16[2,2,32,1024]{3,2,1,0:T(8,128)(2,1)}, f32[2,8,128]{2,1,0:T(8,128)}) custom-call(bf16[4,2,1024]{2,1,0:T(2,128)(2,1)} %bitcast.5, f32[4]{0:T(128)} %weight_hbm.1, s32[1,2]{1,0:T(1,128)} %owners_hbm.1, s32[1,2,2]{2,1,0:T(2,128)} %rotations_hbm.1, bf16[16,16,1024]{2,1,0:T(8,128)(2,1)} %bitcast.3, ...), custom_call_target="tpu_custom_call" | custom-call | flops 6000000000 | bytes 12582912 | tf_op jit(solution)/shard_map/pallas_call | solution.py:533
  62.5 1.7 %shard_map.131 = (bf16[2,2,32,1024]{3,2,1,0:T(8,128)(2,1)}, f32[1,1,2,2]{3,2,1,0:T(2,128)}, f32[1,2,2]{2,1,0:T(2,128)}) custom-call(bf16[2,2,32,1024]{3,2,1,0:T(8,128)(2,1)} %get-tuple-element.8.scores_in, f32[2,8,128]{2,1,0:T(8,128)} %get-tuple-element.9.tops_in), custom_call_target="tpu_custom_call" | custom-call | bytes 524288 | tf_op jit(solution)/shard_map/pallas_call | solution.py:599
